TPU v7x, 256 devices: a whole 4x4x8 slice. The times are simulated.
256 devices in a mesh: dp: 32 (over y, x, core), tensor: 8 (over z).
Axes of the slice: x: 4, y: 4, z: 8, core: 2. Of those that a mesh axis runs over, the one named last changes fastest.
Arguments:
- tokens: bfloat16 [24576, 8192], P('dp', 'tensor'), may hold values from -6 to 6
- frozen_weight: bfloat16 [8192, 2048], P('tensor'), may hold values from -0.0625 to 0.0625
- cotangent: bfloat16 [24576, 2048], P('dp', 'tensor'), may hold values from -1.5 to 1.5
- adapter_down_maps: bfloat16 [64, 8192, 64], P('dp', 'tensor'), may hold values from -0.0625 to 0.0625
- adapter_up_maps: bfloat16 [64, 64, 2048], P('dp', None, 'tensor'), may hold values from -0.75 to 0.75
- tenant_stored_row: int32 [64], replicated, may hold values from 0 to 63, as said below
- tenant_per_block: int32 [192], P('dp'), may hold values from 0 to 63, as said below
- block_padding_rows: int32 [192], P('dp'), may hold values from 0 to 64
Outputs:
- kv_out: bfloat16 [24576, 2048], P('dp', 'tensor')
- grad_tokens: bfloat16 [24576, 8192], P('dp', 'tensor')
- grad_down: bfloat16 [64, 8192, 64], P('dp', 'tensor')
- grad_up: bfloat16 [64, 64, 2048], P('dp', None, 'tensor')
Inputs may be any that keep to these rules, and one draw needn't show every extreme that they name: A permutation: tenant t's adapters are row tenant_stored_row[t] of adapter_down_maps and adapter_up_maps. `tenant_per_block`: the 6 blocks of one dp index name tenants t whose values tenant_stored_row[t] // 2 are 6 different dp indices.
All inputs are finite; a program needn't handle non-finite values.
Results may differ from a plain program's by a relative error of at most 0.023.
Values may be sent and summed in bfloat16 or wider, within the bound.
A program may use at most 128 MiB of HBM per device.

v0:
```python
import jax
import jax.numpy as jnp
from jax import lax
from jax.sharding import PartitionSpec as P


def add_columns(cot_piece, weight_rows):
    return lax.dot_general(
        cot_piece, weight_rows, (((1,), (1,)), ((), ())), preferred_element_type=jnp.float32
    )


def local(
    tokens,
    frozen_weight,
    cotangent,
    adapter_down_maps,
    adapter_up_maps,
    tenant_stored_row,
    tenant_per_block,
    block_padding_rows,
):
    peer_count = lax.axis_size("dp")
    resident_count = adapter_down_maps.shape[0]
    blocks = tenant_per_block.shape[0]
    row_count = tokens.shape[0]
    block_rows = row_count // blocks
    slot_of = jnp.take(tenant_stored_row, tenant_per_block)
    owner_of = slot_of // resident_count
    local_of = slot_of % resident_count
    peer_ids = jnp.arange(peer_count, dtype=jnp.int32)
    matches = owner_of[None, :] == peer_ids[:, None]
    wanted = jnp.sum(jnp.where(matches, local_of[None, :] + 1, 0), axis=1) - 1
    requested = lax.all_to_all(wanted[:, None], "dp", split_axis=0, concat_axis=0, tiled=True)[:, 0]
    picked_tenant = jnp.maximum(requested, 0)
    selected_down = jnp.take(adapter_down_maps, picked_tenant, axis=0)
    selected_up = jnp.take(adapter_up_maps, picked_tenant, axis=0)
    got_down, got_up = (
        lax.all_to_all(selected_down, "dp", split_axis=0, concat_axis=0, tiled=True),
        lax.all_to_all(selected_up, "dp", split_axis=0, concat_axis=0, tiled=True),
    )
    down_panels = jnp.take(got_down, owner_of, axis=0)
    up_panels = jnp.take(got_up, owner_of, axis=0)
    position = jnp.arange(block_rows, dtype=jnp.int32)
    live_rows = (position[None, :] < (block_rows - block_padding_rows)[:, None]).astype(
        jnp.float32
    )[:, :, None]
    token_blocks = tokens.reshape(blocks, block_rows, tokens.shape[1])
    base_out = lax.psum_scatter(
        jnp.dot(tokens, frozen_weight, preferred_element_type=jnp.float32).astype(jnp.bfloat16),
        "tensor",
        scatter_dimension=1,
        tiled=True,
    ).astype(jnp.float32)
    low_part = jnp.einsum(
        "bnd,bdr->bnr", token_blocks, down_panels, preferred_element_type=jnp.float32
    )
    low_rank = lax.psum(low_part.astype(jnp.bfloat16), "tensor")
    low_lift = jnp.einsum("bnr,brc->bnc", low_rank, up_panels, preferred_element_type=jnp.float32)
    kv_blocks = live_rows * (
        base_out.reshape(blocks, block_rows, base_out.shape[1]) + 0.5 * low_lift
    )
    kv_out = kv_blocks.astype(jnp.bfloat16).reshape(row_count, base_out.shape[1])
    grad_rows = (
        cotangent.reshape(blocks, block_rows, cotangent.shape[1]).astype(jnp.float32) * live_rows
    ).astype(jnp.bfloat16)
    back_part = jnp.einsum("bnc,brc->bnr", grad_rows, up_panels, preferred_element_type=jnp.float32)
    back_low = (
        0.5 * lax.psum(back_part.astype(jnp.bfloat16), "tensor").astype(jnp.float32)
    ).astype(jnp.bfloat16)
    flat_grad = grad_rows.reshape(row_count, cotangent.shape[1])
    base_grad = add_columns(
        lax.all_gather(flat_grad, "tensor", axis=1, tiled=True), weight_rows=frozen_weight
    )
    side_grad = jnp.einsum(
        "bnr,bdr->bnd", back_low, down_panels, preferred_element_type=jnp.float32
    )
    grad_tokens = (base_grad + side_grad.reshape(row_count, tokens.shape[1])).astype(jnp.bfloat16)
    down_term = jnp.einsum(
        "bnd,bnr->bdr", token_blocks, back_low, preferred_element_type=jnp.float32
    ).astype(jnp.bfloat16)
    up_term = (
        0.5 * jnp.einsum("bnr,bnc->brc", low_rank, grad_rows, preferred_element_type=jnp.float32)
    ).astype(jnp.bfloat16)
    send_down = (
        jnp.zeros((peer_count,) + down_term.shape[1:], jnp.bfloat16).at[owner_of].set(down_term)
    )
    send_up = jnp.zeros((peer_count,) + up_term.shape[1:], jnp.bfloat16).at[owner_of].set(up_term)
    back_down_terms, back_up_terms = (
        lax.all_to_all(send_down, "dp", split_axis=0, concat_axis=0, tiled=True),
        lax.all_to_all(send_up, "dp", split_axis=0, concat_axis=0, tiled=True),
    )
    held_ids = jnp.arange(resident_count, dtype=jnp.int32)
    onehot = (requested[None, :] == held_ids[:, None]).astype(jnp.bfloat16)
    grad_down = jnp.einsum(
        "hp,pdr->hdr", onehot, back_down_terms, preferred_element_type=jnp.float32
    ).astype(jnp.bfloat16)
    grad_up = jnp.einsum(
        "hp,prc->hrc", onehot, back_up_terms, preferred_element_type=jnp.float32
    ).astype(jnp.bfloat16)
    return (kv_out, grad_tokens, grad_down, grad_up)


def solution(mesh):
    placed = (
        P("dp", "tensor"),
        P("tensor", None),
        P("dp", "tensor"),
        P("dp", "tensor", None),
        P("dp", None, "tensor"),
        P(),
        P("dp"),
        P("dp"),
    )
    return jax.shard_map(
        local,
        mesh=mesh,
        in_specs=placed,
        out_specs=(
            P("dp", "tensor"),
            P("dp", "tensor"),
            P("dp", "tensor", None),
            P("dp", None, "tensor"),
        ),
        check_vma=False,
    )
```

profile of v0, /device:TPU:1, one launch (start us, length us, event | category | flops | bytes accessed | tf_op | source)
XLA Modules:
  0.0 301.6 jit_solution(3719929188025807128)
XLA Ops:
  7.2 0.0 copy-start
  7.2 0.8 compare_select_fusion.1
  8.0 1.3 gather_fusion
  9.3 0.7 compare_and_fusion
  10.0 0.1 select_reduce_fusion
  10.0 0.1 copy.29
  10.1 15.3 %all_to_all.29 = s32[32,1,1]{2,1,0:T(1,128)S(1)} all-to-all(s32[32,1,1]{2,1,0:T(1,128)S(1)} %copy.29), channel_id=1, replica_groups=mesh['dp'=32,'tensor'=8] {'dp'}, dimensions={0} | all-to-all | bytes 256 | tf_op jit(solution)/shard_map/all_to_all | solution.py:34
  25.5 1.2 fusion.27
  26.7 1.5 gather_fusion.3
  28.2 1.1 broadcast_select_fusion.1
  29.4 4.9 %all-to-all-start.2 = ((bf16[32,64,256]{2,1,0:T(8,128)(2,1)}), bf16[32,64,256]{2,1,0:T(8,128)(2,1)}, u32[]{:S(2)}, u32[]{:S(2)}) async-start(bf16[32,64,256]{2,1,0:T(8,128)(2,1)} %broadcast_select_fusion.1), calls=%async_computation.3 | async-start | bytes 2097152 | tf_op jit(solution)/shard_map/all_to_all | solution.py:40
  34.3 2.8 gather_fusion.1
  37.1 4.6 %broadcast_select_fusion = bf16[32,1024,64]{1,2,0:T(8,128)(2,1)} fusion(bf16[32,1024,64]{1,2,0:T(8,128)(2,1)} %gather_fusion.1, pred[32]{0:T(512)(128)(4,1)S(1)} %maximum_compare_fusion), kind=kLoop, calls=%fused_computation.9 | loop fusion | flops 2097152 | bytes 8388640 | tf_op jit(solution)/shard_map/jit(_take)/select_n | solution.py:36
  41.7 9.9 %all-to-all-done.2 = bf16[32,64,256]{2,1,0:T(8,128)(2,1)} async-done(((bf16[32,64,256]{2,1,0:T(8,128)(2,1)}), bf16[32,64,256]{2,1,0:T(8,128)(2,1)}, u32[]{:S(2)}, u32[]{:S(2)}) %all-to-all-start.2) | async-done | bytes 1048608 | tf_op jit(solution)/shard_map/all_to_all | solution.py:40
  51.6 4.8 %all-to-all-start.1 = ((bf16[32,1024,64]{1,2,0:T(8,128)(2,1)}), bf16[32,1024,64]{1,2,0:T(8,128)(2,1)}, u32[]{:S(2)}, u32[]{:S(2)}) async-start(bf16[32,1024,64]{1,2,0:T(8,128)(2,1)} %broadcast_select_fusion), calls=%async_computation.2 | async-start | bytes 8388608 | tf_op jit(solution)/shard_map/all_to_all | solution.py:39
  56.4 0.0 all-reduce.3.cloned.1.call-start
  56.5 0.1 fusion.17
  56.6 1.8 gather_fusion.4
  58.4 1.0 convolution_convert_fusion.2
  59.4 47.4 %all-to-all-done.1 = bf16[32,1024,64]{1,2,0:T(8,128)(2,1)} async-done(((bf16[32,1024,64]{1,2,0:T(8,128)(2,1)}), bf16[32,1024,64]{1,2,0:T(8,128)(2,1)}, u32[]{:S(2)}, u32[]{:S(2)}) %all-to-all-start.1) | async-done | bytes 4194336 | tf_op jit(solution)/shard_map/all_to_all | solution.py:39
  106.8 2.8 gather_fusion.2
  109.6 1.3 fusion.11
  111.0 0.0 all-reduce.3.cloned.1.call-update
  111.0 0.0 all-gather.2.cloned.1.call-start
  111.0 0.9 multiply_convert_fusion.1
  112.0 0.0 all-gather.2.cloned.1.call-update
  112.0 0.0 reduce-scatter.2.cloned.1.call-start
  112.0 6.9 %convolution_convert_fusion = bf16[768,2048]{1,0:T(8,128)(2,1)} fusion(bf16[768,1024]{1,0:T(8,128)(2,1)S(1)} %copy-done, bf16[1024,2048]{1,0:T(8,128)(2,1)} %param.9), kind=kOutput, calls=%fused_computation.10 | convolution fusion | flops 3222798336 | bytes 8912896 | tf_op jit(solution)/shard_map/dot_general | solution.py:50
  119.0 0.0 reduce-scatter.2.cloned.1.call-update
  119.0 60.7 %all-reduce.3.cloned.1.call-done = (bf16[6,128,64]{1,2,0:T(8,128)(2,1)}, bf16[6,128,64]{1,2,0:T(8,128)(2,1)}) async-done(((bf16[6,128,64]{1,2,0:T(8,128)(2,1)}, bf16[6,128,64]{1,2,0:T(8,128)(2,1)}), (bf16[6,128,64]{1,2,0:T(8,128)(2,1)}, bf16[6,128,64]{1,2,0:T(8,128)(2,1)})) %all-reduce.3.cloned.1.call-update) | async-done | bytes 196624 | tf_op jit(solution)/shard_map/psum | solution.py:58
  179.7 1.2 fusion.10
  181.0 1.1 broadcast_in_dim.84
  182.1 2.1 scatter_fusion.1
  184.2 12.6 %all-to-all-start.4 = ((bf16[32,64,256]{2,1,0:T(8,128)(2,1)}), bf16[32,64,256]{2,1,0:T(8,128)(2,1)S(1)}, u32[]{:S(2)}, u32[]{:S(2)}) async-start(bf16[32,64,256]{2,1,0:T(8,128)(2,1)} %scatter_fusion.1), calls=%async_computation.5 | async-start | bytes 2097152 | tf_op jit(solution)/shard_map/all_to_all | solution.py:91
  196.8 1.3 fusion.3
  198.1 2.5 broadcast_in_dim.83
  200.6 3.1 %scatter_fusion = bf16[32,1024,64]{1,2,0:T(8,128)(2,1)} fusion(bf16[32,1024,64]{1,2,0:T(8,128)(2,1)} %broadcast_in_dim.83, s32[6]{0:T(128)S(1)} %compare_select_fusion, bf16[6,1024,64]{1,2,0:T(8,128)(2,1)} %fusion.3), kind=kCustom, calls=%fused_computation.5 | custom fusion | bytes 2359320 | tf_op jit(solution)/shard_map/scatter | solution.py:86
  203.6 10.4 %all-to-all-done.4 = bf16[32,64,256]{2,1,0:T(8,128)(2,1)S(1)} async-done(((bf16[32,64,256]{2,1,0:T(8,128)(2,1)}), bf16[32,64,256]{2,1,0:T(8,128)(2,1)S(1)}, u32[]{:S(2)}, u32[]{:S(2)}) %all-to-all-start.4) | async-done | bytes 1048608 | tf_op jit(solution)/shard_map/all_to_all | solution.py:91
  214.0 4.8 %all-to-all-start.3 = ((bf16[32,1024,64]{1,2,0:T(8,128)(2,1)}), bf16[32,1024,64]{1,2,0:T(8,128)(2,1)}, u32[]{:S(2)}, u32[]{:S(2)}) async-start(bf16[32,1024,64]{1,2,0:T(8,128)(2,1)} %scatter_fusion), calls=%async_computation.4 | async-start | bytes 8388608 | tf_op jit(solution)/shard_map/all_to_all | solution.py:90
  218.8 2.3 fusion.13
  221.1 0.7 convolution_convert_fusion.4
  221.8 0.6 copy.33
  222.4 15.1 %all-gather.2.cloned.1.call-done = bf16[768,2048]{1,0:T(8,128)(2,1)} async-done(((bf16[768,256]{1,0:T(8,128)(2,1)}), bf16[768,2048]{1,0:T(8,128)(2,1)}) %all-gather.2.cloned.1.call-update) | async-done | bytes 3145744 | tf_op jit(solution)/shard_map/all_gather | solution.py:73
  237.5 8.7 %fusion.2 = bf16[768,1024]{1,0:T(8,128)(2,1)} fusion(f32[6,128,1024]{2,1,0:T(8,128)} %fusion.13, bf16[768,2048]{1,0:T(8,128)(2,1)} %all-gather.2.cloned.1.call-done, bf16[1024,2048]{1,0:T(8,128)(2,1)} %param.9), kind=kOutput, calls=%fused_computation.12 | convolution fusion | flops 3222798336 | bytes 12058624 | tf_op jit(solution)/shard_map/dot_general | solution.py:8
  246.2 39.3 %reduce-scatter.2.cloned.1.call-done = bf16[768,256]{1,0:T(8,128)(2,1)} async-done(((bf16[768,2048]{1,0:T(8,128)(2,1)}), bf16[768,256]{1,0:T(8,128)(2,1)}) %reduce-scatter.2.cloned.1.call-update) | async-done | bytes 393232 | tf_op jit(solution)/shard_map/reduce_scatter | solution.py:49
  285.5 2.1 fusion.6
  287.6 6.8 %fusion.7 = bf16[2,1024,64]{1,0,2:T(2,128)(2,1)S(1)} fusion(bf16[32,1024,64]{1,2,0:T(8,128)(2,1)} %all-to-all-done.3, s32[32]{0:T(128)S(1)} %get-tuple-element.24), kind=kOutput, calls=%fused_computation.19 | convolution fusion | flops 8519744 | bytes 4456576 | tf_op jit(solution)/shard_map/hp,pdr->hdr/dot_general | solution.py:95
  294.3 0.8 copy.32
  (24 shorter events, 0.1 us)
Async XLA Ops:
  7.2 102.4 %copy-start = (bf16[768,1024]{1,0:T(8,128)(2,1)S(1)}, bf16[768,1024]{1,0:T(8,128)(2,1)}, u32[]{:S(2)}) copy-start(bf16[768,1024]{1,0:T(8,128)(2,1)} %param.8) | copy-start | bytes 4718596
  26.7 7.5 %copy-start.1 = (bf16[2,1024,64]{1,2,0:T(8,128)(2,1)S(1)}, bf16[2,1024,64]{1,2,0:T(8,128)(2,1)}, u32[]{:S(2)}) copy-start(bf16[2,1024,64]{1,2,0:T(8,128)(2,1)} %param.11) | copy-start | bytes 786436
  29.4 22.2 %all-to-all-start.2 = ((bf16[32,64,256]{2,1,0:T(8,128)(2,1)}), bf16[32,64,256]{2,1,0:T(8,128)(2,1)}, u32[]{:S(2)}, u32[]{:S(2)}) async-start(bf16[32,64,256]{2,1,0:T(8,128)(2,1)} %broadcast_select_fusion.1), calls=%async_computation.3 | async-start | bytes 2097152 | tf_op jit(solution)/shard_map/all_to_all | solution.py:40
  41.7 14.8 %copy-start.7 = (s32[6]{0:T(128)S(1)}, s32[6]{0:T(128)}, u32[]{:S(2)}) copy-start(s32[6]{0:T(128)} %param.15) | copy-start | bytes 76
  41.7 16.7 %copy-start.2 = (bf16[768,256]{1,0:T(8,128)(2,1)S(1)}, bf16[768,256]{1,0:T(8,128)(2,1)}, u32[]{:S(2)}) copy-start(bf16[768,256]{1,0:T(8,128)(2,1)} %param.10) | copy-start | bytes 1179652
  51.6 55.2 %all-to-all-start.1 = ((bf16[32,1024,64]{1,2,0:T(8,128)(2,1)}), bf16[32,1024,64]{1,2,0:T(8,128)(2,1)}, u32[]{:S(2)}, u32[]{:S(2)}) async-start(bf16[32,1024,64]{1,2,0:T(8,128)(2,1)} %broadcast_select_fusion), calls=%async_computation.2 | async-start | bytes 8388608 | tf_op jit(solution)/shard_map/all_to_all | solution.py:39
  56.4 123.3 %all-reduce.3.cloned.1.call-start = ((), (), s32[]{:S(2)}) async-start(), calls=%async_computation.8 | async-start | bytes 393216 | tf_op jit(solution)/shard_map/psum | solution.py:58
  58.4 1.0 copy-start.4
  111.0 126.6 %all-gather.2.cloned.1.call-start = ((), (), s32[]{:S(2)}) async-start(), calls=%async_computation.7 | async-start | bytes 3538944 | tf_op jit(solution)/shard_map/all_gather | solution.py:73
  112.0 173.5 %reduce-scatter.2.cloned.1.call-start = ((), (), s32[]{:S(2)}) async-start(), calls=%async_computation.6 | async-start | bytes 3538944 | tf_op jit(solution)/shard_map/reduce_scatter | solution.py:49
  179.7 17.1 %copy-start.3 = (bf16[6,128,64]{1,2,0:T(8,128)(2,1)S(1)}, bf16[6,128,64]{1,2,0:T(8,128)(2,1)}, u32[]{:S(2)}) copy-start(bf16[6,128,64]{1,2,0:T(8,128)(2,1)} %get-tuple-element.27) | copy-start | bytes 294916
  184.2 29.7 %all-to-all-start.4 = ((bf16[32,64,256]{2,1,0:T(8,128)(2,1)}), bf16[32,64,256]{2,1,0:T(8,128)(2,1)S(1)}, u32[]{:S(2)}, u32[]{:S(2)}) async-start(bf16[32,64,256]{2,1,0:T(8,128)(2,1)} %scatter_fusion.1), calls=%async_computation.5 | async-start | bytes 2097152 | tf_op jit(solution)/shard_map/all_to_all | solution.py:91
  214.0 73.6 %all-to-all-start.3 = ((bf16[32,1024,64]{1,2,0:T(8,128)(2,1)}), bf16[32,1024,64]{1,2,0:T(8,128)(2,1)}, u32[]{:S(2)}, u32[]{:S(2)}) async-start(bf16[32,1024,64]{1,2,0:T(8,128)(2,1)} %scatter_fusion), calls=%async_computation.4 | async-start | bytes 8388608 | tf_op jit(solution)/shard_map/all_to_all | solution.py:90
  222.4 63.1 %copy-start.5 = (bf16[6,64,256]{2,1,0:T(8,128)(2,1)S(1)}, bf16[6,64,256]{2,1,0:T(8,128)(2,1)}, u32[]{:S(2)}) copy-start(bf16[6,64,256]{2,1,0:T(8,128)(2,1)} %copy-done.4) | copy-start | bytes 589828
  222.4 63.1 %copy-start.6 = (bf16[6,128,64]{1,2,0:T(8,128)(2,1)S(1)}, bf16[6,128,64]{1,2,0:T(8,128)(2,1)}, u32[]{:S(2)}) copy-start(bf16[6,128,64]{1,2,0:T(8,128)(2,1)} %get-tuple-element.26) | copy-start | bytes 294916
Sparse Core Ops, SparseCore 0:
  111.1 68.5 all-reduce.2
  182.1 55.3 all-gather.1
  240.3 45.1 reduce-scatter.1
where the time goes:
time: 304 us; the launch traced here: 302 us
  waiting for transfers between devices  183 us (60%)
  matrix products  32.2 us (11%)
  starting transfers between devices  27.2 us (9%)
  local copies, waits for them, and re-layouts  20.5 us (7%)
  blocking collectives  15.3 us (5%)
  between operations  13.9 us (5%)
  other arithmetic  9.57 us (3%)
    psum x1, waiting for transfers between devices, local(): low_rank = lax.psum(low_part.astype(jnp.bfloat16), 'tensor')  60.7 us
    all_to_all x1, waiting for transfers between devices, local(): lax.all_to_all(selected_down, 'dp', split_axis=0, concat_axis=0, tiled=True)  47.4 us
    reduce_scatter x1, waiting for transfers between devices, local(): lax.psum_scatter(jnp.dot(tokens, frozen_weight, preferred_element_type=jn...  39.3 us
    all_to_all x1, blocking collectives, local(): lax.all_to_all(wanted[:, None], 'dp', split_axis=0, concat_axis=0, tiled=...  15.3 us
    all_gather x1, waiting for transfers between devices, local(): lax.all_gather(flat_grad, 'tensor', axis=1, tiled=True)  15.1 us
    all_to_all x1, starting transfers between devices, local(): lax.all_to_all(send_up, 'dp', split_axis=0, concat_axis=0, tiled=True)  12.6 us
    all_to_all x1, waiting for transfers between devices, local(): lax.all_to_all(send_up, 'dp', split_axis=0, concat_axis=0, tiled=True)  10.4 us
    all_to_all x1, waiting for transfers between devices, local(): lax.all_to_all(selected_up, 'dp', split_axis=0, concat_axis=0, tiled=True)  9.92 us
  transfers between devices with their start and end apart: 7, of which 6 were waited for; matrix products, arithmetic and copies ran while one was open for 14% of the time, Pallas kernels for 0%

commit v1 on v0

v1 whole, which is shorter than its diff:
```python
import jax
import jax.numpy as jnp
from jax import lax
from jax.experimental import pallas as pl
from jax.experimental.pallas import tpu as pltpu
from jax.sharding import PartitionSpec as P

MESH = pl.DeviceIdType.MESH
F32, BF16, I32 = jnp.float32, jnp.bfloat16, jnp.int32
NT = (((1,), (1,)), ((), ()))
TN = (((0,), (0,)), ((), ()))
NZ, NB, BR = 8, 6, 128
ROWS, HALF = 768, 384
FEAT, COLS, RANK, HR = 1024, 256, 64, 32
N_SEM = 160


def mm(a, b, dims=None):
    if dims is None:
        return jnp.dot(a, b, preferred_element_type=F32)
    return lax.dot_general(a, b, dims, preferred_element_type=F32)


def kernel(
    stored, tenants, padding, tok_in, w_in, cot_in, down_in, up_in,
    kv_out, gt_out, gd_out, gu_out,
    tok, w, g, acc, rs_right, rs_left, rs_first, kv, gt,
    ad, au, dsel, usel, dsib, usib, ints, ints_smem, table,
    low_part, low_recv, low, back_part, back_recv, back,
    td, tu, rd, ru, qd, qu, qd_in, qu_in, fd, fu, fd_in, fu_in,
    send_sem, recv_sem, load_sem, store_sem, copy_sem,
):
    dp, z = lax.axis_index("dp"), lax.axis_index("tensor")
    y, x, c = dp // 8, (dp // 2) % 4, dp % 2
    mp, mq = (1 - c) * x + c * y, (1 - c) * y + c * x

    def z_at(step):
        return (dp, (z + step + NZ) % NZ)

    def p_at(step):
        return (((y + c * step + 4) % 4) * 8 + ((x + (1 - c) * step + 4) % 4) * 2 + c, z)

    def q_at(step):
        return (((y + (1 - c) * step + 4) % 4) * 8 + ((x + c * step + 4) % 4) * 2 + c, z)

    sibling = (dp + 1 - 2 * c, z)
    sent = {}

    def send(key, src, dst, device):
        n = len(sent)
        copy = pltpu.make_async_remote_copy(
            src_ref=src, dst_ref=dst, send_sem=send_sem.at[n], recv_sem=recv_sem.at[n],
            device_id=device, device_id_type=MESH,
        )
        copy.start()
        sent[key] = copy

    def recv(key):
        sent[key].wait_recv()

    loads = {}

    def load(key, src, dst):
        loads[key] = pltpu.make_async_copy(src, dst, load_sem.at[len(loads)])
        loads[key].start()

    load("g", cot_in, g.at[0])
    load("u", up_in.at[:, pl.ds(c * HR, HR)], au.at[0, 0, pl.ds(2 * c, 2)])
    load("d", down_in.at[:, pl.ds(c * HR, HR)], ad.at[0, 0, pl.ds(2 * c, 2)])
    load("tok", tok_in, tok)

    def load_w(k):
        load(("w", k), w_in.at[:, pl.ds(((z + k) % NZ) * COLS, COLS)], w.at[k])

    for k in (4, 3, 5, 0, 2, 6, 1, 7):
        load_w(k)

    barrier = pltpu.get_barrier_semaphore()
    friends = [z_at(k) for k in range(1, NZ)] + [p_at(1), p_at(-1), q_at(1), q_at(-1), sibling]
    for friend in friends:
        pl.semaphore_signal(barrier, inc=1, device_id=friend, device_id_type=MESH)

    lane = lax.broadcasted_iota(I32, (8, 128), 1)
    mine = jnp.zeros((8, 128), I32)
    for b in range(NB):
        mine = jnp.where(lane == b, stored[tenants[b]], mine)
    ints[0, c] = mine

    loads["g"].wait()
    position = lax.broadcasted_iota(I32, (BR, 1), 0)

    def live(b):
        return (position < BR - padding[b]).astype(F32)

    for b in range(NB):
        rows = pl.ds(b * BR, BR)
        g[0, rows] = (g[0, rows].astype(F32) * live(b)).astype(BF16)

    pl.semaphore_wait(barrier, len(friends))

    half = (pl.ds(0, HALF), pl.ds(HALF, HALF))

    def ag_send(step, h, right):
        src, dst = ((-step) % NZ, (-step - 1) % NZ) if right else (step, step + 1)
        send(("ag", right, step, h), g.at[src, half[h]], g.at[dst, half[h]], z_at(1 if right else -1))

    def ag_pass(step, h, right):
        recv(("ag", right, step, h))
        ag_send(step + 1, h, right)

    for h in (0, 1):
        ag_send(0, h, True)
        ag_send(0, h, False)

    send("f0i", ints.at[0, c], ints.at[0, c], sibling)
    send("f0u", up_in.at[:, pl.ds((1 - c) * HR, HR)], au.at[0, 0, pl.ds(2 * c, 2)], sibling)
    send("f0d", down_in.at[:, pl.ds((1 - c) * HR, HR)], ad.at[0, 0, pl.ds(2 * c, 2)], sibling)

    def partial(k, h):
        return mm(tok[half[h]], w[k])

    def rs_start(step, h, right):
        k = (4 - step) if right else (4 + step)
        slot = step * 2 + (0 if right else 1)
        rs_first[slot] = partial(k, h).astype(BF16)
        dst = rs_right if right else rs_left
        send(("rs", right, step, h), rs_first.at[slot], dst.at[step, half[h]], z_at(1 if right else -1))

    def rs_pass(step, h, right):
        k = (4 - step) if right else (4 + step)
        buf = rs_right if right else rs_left
        own = partial(k, h)
        recv(("rs", right, step - 1, h))
        buf[step - 1, half[h]] = (buf[step - 1, half[h]].astype(F32) + own).astype(BF16)
        send(("rs", right, step, h), buf.at[step - 1, half[h]], buf.at[step, half[h]], z_at(1 if right else -1))

    loads["tok"].wait()
    loads[("w", 4)].wait()
    rs_start(0, 0, True)
    rs_start(0, 1, False)
    loads[("w", 3)].wait()
    rs_start(1, 1, True)
    loads[("w", 5)].wait()
    rs_start(1, 0, False)

    def f1_send(name, a):
        send((name, "f1", 1), a.at[0, 0], a.at[0, 3], p_at(1))
        send((name, "f1", -1), a.at[0, 0], a.at[0, 1], p_at(-1))

    def f1_pass(name, a):
        recv((name, "f1", 1))
        send((name, "f1x", 1), a.at[0, 3, pl.ds(0, 2)], a.at[0, 2, pl.ds(0, 2)], p_at(1))
        recv((name, "f1", -1))
        send((name, "f1x", -1), a.at[0, 1, pl.ds(2, 2)], a.at[0, 2, pl.ds(2, 2)], p_at(-1))

    def f1_end(name):
        recv((name, "f1x", 1))
        recv((name, "f1x", -1))

    def f2_send(name, a, rp):
        send((name, "f2", 1, rp), a.at[0, rp], a.at[3, rp], q_at(1))
        send((name, "f2", -1, rp), a.at[0, rp], a.at[1, rp], q_at(-1))

    def f2_pass(name, a, rp):
        recv((name, "f2", 1, rp))
        send((name, "f2x", 1, rp), a.at[3, rp, pl.ds(0, 2)], a.at[2, rp, pl.ds(0, 2)], q_at(1))
        recv((name, "f2", -1, rp))
        send((name, "f2x", -1, rp), a.at[1, rp, pl.ds(2, 2)], a.at[2, rp, pl.ds(2, 2)], q_at(-1))

    def f2_end(name):
        for rp in range(4):
            recv((name, "f2x", 1, rp))
            recv((name, "f2x", -1, rp))

    loads["u"].wait()
    recv("f0u")
    f1_send("u", au)
    f2_send("u", au, 0)
    recv("f0i")
    send(("i", 1), ints.at[0], ints.at[3], q_at(1))
    send(("i", -1), ints.at[0], ints.at[1], q_at(-1))
    loads["d"].wait()
    recv("f0d")
    f1_send("d", ad)
    f2_send("d", ad, 0)
    f1_pass("u", au)
    f2_send("u", au, 3)
    f2_send("u", au, 1)
    recv(("i", 1))
    send(("i", 2), ints.at[3], ints.at[2], q_at(1))
    recv(("i", -1))
    f1_end("u")
    f2_send("u", au, 2)
    f2_pass("u", au, 0)
    f1_pass("d", ad)
    f2_send("d", ad, 3)
    f2_send("d", ad, 1)

    def acc_first():
        def body(i, _):
            rows = pl.ds(i * 256, 256)
            acc[rows] = mm(g[0, rows], w[0], NT)
            return 0

        lax.fori_loop(0, 3, body, 0)

    def acc_pair(k):
        def body(i, _):
            rows = pl.ds(i * 256, 256)
            acc[rows] += mm(g[k, rows], w[k], NT) + mm(g[NZ - k, rows], w[NZ - k], NT)
            return 0

        lax.fori_loop(0, 3, body, 0)

    loads[("w", 0)].wait()
    acc_first()
    f2_pass("u", au, 3)
    f2_pass("u", au, 1)
    f2_pass("u", au, 2)
    recv(("i", 2))
    to_smem = pltpu.make_async_copy(ints, ints_smem, copy_sem.at[0])
    to_smem.start()
    to_smem.wait()

    def place(slot):
        chip, inner = slot // 4, slot % 4
        cy, cx = chip // 4, chip % 4
        rq = ((1 - c) * cy + c * cx - mq + 4) % 4
        rp = ((1 - c) * cx + c * cy - mp + 4) % 4
        return rq, rp, inner

    def pick(name, a, sel, sib):
        for b in range(NB):
            rq, rp, inner = place(ints_smem[0, 1 - c, 0, b])
            sib[b] = a[rq, rp, inner]
        send((name, "sib"), sib, sel.at[c], sibling)
        for b in range(NB):
            rq, rp, inner = place(ints_smem[0, c, 0, b])
            sel[c, b] = a[rq, rp, inner]

    def panel(sel, b):
        return jnp.concatenate([sel[0, b], sel[1, b]], axis=0)

    def sum_scatter(name, part, got):
        for k in range(1, NZ):
            rows = pl.ds(((z + k) % NZ) * 48, 48)
            send((name, "s", k), part.at[rows], got.at[k], z_at(k))

    def sum_gather(name, part, got, total, scale):
        own = pl.ds(z * 48, 48)
        value = part[own].astype(F32)
        for k in range(1, NZ):
            recv((name, "s", k))
            value = value + got[k].astype(F32)
        total[own] = (value * scale).astype(BF16)
        for k in range(1, NZ):
            send((name, "g", k), total.at[own], total.at[own], z_at(k))

    def sum_end(name):
        for k in range(1, NZ):
            recv((name, "g", k))

    for h in (0, 1):
        ag_pass(0, h, True)
        ag_pass(0, h, False)
    f2_end("u")
    pick("u", au, usel, usib)
    recv(("u", "sib"))
    for b in range(NB):
        back_part[pl.ds(b * RANK, RANK)] = mm(panel(usel, b), g[0, pl.ds(b * BR, BR)], NT).astype(BF16)
    sum_scatter("back", back_part, back_recv)
    loads[("w", 2)].wait()
    loads[("w", 6)].wait()
    loads[("w", 1)].wait()
    loads[("w", 7)].wait()
    f1_end("d")
    f2_send("d", ad, 2)
    f2_pass("d", ad, 0)
    rs_pass(1, 0, True)
    rs_pass(1, 1, False)
    f2_pass("d", ad, 3)
    f2_pass("d", ad, 1)
    sum_gather("back", back_part, back_recv, back, 0.5)
    acc_pair(1)

    def fill_table(j, _):
        pj = (mp + j // 4) % 4
        slot = (((1 - c) * mq + c * pj) * 4 + (1 - c) * pj + c * mq) * 4 + j % 4
        for i in range(4):
            for core in range(2):
                entry = I32(48)
                for b in range(NB):
                    entry = jnp.where(ints_smem[i, core, 0, b] == slot, (i * 2 + core) * NB + b, entry)
                table[j, i * 2 + core] = entry
        return 0

    lax.fori_loop(0, 16, fill_table, 0)
    rd[48] = jnp.zeros((HR, FEAT), BF16)
    ru[48] = jnp.zeros((HR, COLS), BF16)

    for h in (0, 1):
        ag_pass(1, h, True)
        ag_pass(1, h, False)
    for h in (0, 1):
        rs_pass(2, h, True)
        rs_pass(2, h, False)

    def terms_out(name, t, r, sem):
        send((name, "t0"), t.at[1 - c], r.at[pl.ds(c * NB, NB)], sibling)
        send((name, "t1", 1), t.at[c], r.at[pl.ds(36 + c * NB, NB)], q_at(1))
        send((name, "t1", -1), t.at[c], r.at[pl.ds(12 + c * NB, NB)], q_at(-1))
        own = pltpu.make_async_copy(t.at[c], r.at[pl.ds(c * NB, NB)], copy_sem.at[sem])
        own.start()
        return own

    def terms_sibling(name, t, r):
        recv((name, "t0"))
        other = (1 - c) * NB
        send((name, "t2", 1), r.at[pl.ds(other, NB)], r.at[pl.ds(36 + other, NB)], q_at(1))
        send((name, "t2", -1), r.at[pl.ds(other, NB)], r.at[pl.ds(12 + other, NB)], q_at(-1))

    def terms_pass(name, t, r):
        recv((name, "t1", 1))
        recv((name, "t2", 1))
        send((name, "t3", 1), r.at[pl.ds(36, NB)], r.at[pl.ds(24, NB)], q_at(1))
        recv((name, "t1", -1))
        recv((name, "t2", -1))
        send((name, "t3", -1), r.at[pl.ds(12 + NB, NB)], r.at[pl.ds(24 + NB, NB)], q_at(-1))

    def add_up(r, q, j):
        def body(inner, _):
            total = r[table[j * 4 + inner, 0]].astype(F32)
            for d in range(1, 8):
                total = total + r[table[j * 4 + inner, d]].astype(F32)
            q[j, inner] = total.astype(BF16)
            return 0

        lax.fori_loop(0, 4, body, 0)

    def sums_out(name, r, q, q_in):
        recv((name, "t3", 1))
        recv((name, "t3", -1))
        add_up(r, q, 2)
        send((name, "q0", 1), q.at[2, pl.ds(0, 2)], q_in.at[0, pl.ds(0, 2)], p_at(1))
        send((name, "q0", -1), q.at[2, pl.ds(2, 2)], q_in.at[0, pl.ds(2, 2)], p_at(-1))
        add_up(r, q, 1)
        add_up(r, q, 3)
        add_up(r, q, 0)

    def sums_pass(name, q, q_in):
        recv((name, "q0", 1))
        q[1, 0:2] = (q[1, 0:2].astype(F32) + q_in[0, 0:2].astype(F32)).astype(BF16)
        send((name, "q1", 1), q.at[1], q_in.at[1], p_at(1))
        recv((name, "q0", -1))
        q[3, 2:4] = (q[3, 2:4].astype(F32) + q_in[0, 2:4].astype(F32)).astype(BF16)
        send((name, "q1", -1), q.at[3], q_in.at[2], p_at(-1))

    def sums_end(name, q, q_in, f, f_in):
        recv((name, "q1", 1))
        recv((name, "q1", -1))
        for k in range(4):
            f[k] = (q[0, k].astype(F32) + q_in[1, k].astype(F32) + q_in[2, k].astype(F32)).astype(BF16)
        send((name, "t9"), f.at[pl.ds(2 - 2 * c, 2)], f_in, sibling)

    stores = []

    def store(src, dst):
        stores.append(pltpu.make_async_copy(src, dst, store_sem.at[len(stores)]))
        stores[-1].start()

    def sums_store(name, f, f_in, out):
        store(f.at[pl.ds(2 * c, 2)], out.at[:, pl.ds(c * HR, HR)])
        recv((name, "t9"))
        store(f_in, out.at[:, pl.ds((1 - c) * HR, HR)])

    sum_end("back")
    for b in range(NB):
        term = mm(back[pl.ds(b * RANK, RANK)], tok[pl.ds(b * BR, BR)]).astype(BF16)
        td[0, b] = term[:HR]
        td[1, b] = term[HR:]
    own_d = terms_out("d", td, rd, 1)
    f2_pass("d", ad, 2)
    f2_end("d")
    pick("d", ad, dsel, dsib)
    terms_sibling("d", td, rd)
    recv(("d", "sib"))
    for b in range(NB):
        low_part[pl.ds(b * RANK, RANK)] = mm(panel(dsel, b), tok[pl.ds(b * BR, BR)], NT).astype(BF16)
    sum_scatter("low", low_part, low_recv)
    acc_pair(2)
    ag_pass(2, 0, True)
    ag_pass(2, 1, False)
    sum_gather("low", low_part, low_recv, low, 1.0)
    for h in (0, 1):
        rs_pass(3, h, True)
        rs_pass(3, h, False)
    terms_pass("d", td, rd)
    for b in range(NB):
        rows = pl.ds(b * BR, BR)
        acc[rows] += mm(back[pl.ds(b * RANK, RANK)], panel(dsel, b), TN)
    sum_end("low")
    for b in range(NB):
        term = (0.5 * mm(low[pl.ds(b * RANK, RANK)], g[0, pl.ds(b * BR, BR)])).astype(BF16)
        tu[0, b] = term[:HR]
        tu[1, b] = term[HR:]
    own_u = terms_out("u", tu, ru, 2)
    own_d.wait()
    own_u.wait()
    terms_sibling("u", tu, ru)
    sums_out("d", rd, qd, qd_in)
    terms_pass("u", tu, ru)
    sums_pass("d", qd, qd_in)
    recv(("ag", True, 2, 1))
    recv(("ag", False, 2, 0))
    acc_pair(3)
    sums_out("u", ru, qu, qu_in)
    sums_end("d", qd, qd_in, fd, fd_in)
    sums_pass("u", qu, qu_in)
    sums_store("d", fd, fd_in, gd_out)
    sums_end("u", qu, qu_in, fu, fu_in)

    recv(("ag", True, 3, 0))
    recv(("ag", False, 3, 1))

    def last_rows(i, _):
        rows = pl.ds(i * 256, 256)
        gt[rows] = (acc[rows] + mm(g[4, rows], w[4], NT)).astype(BF16)
        return 0

    lax.fori_loop(0, 3, last_rows, 0)
    store(gt, gt_out)
    sums_store("u", fu, fu_in, gu_out)

    for h in (0, 1):
        base = partial(0, h)
        recv(("rs", True, 3, h))
        recv(("rs", False, 3, h))
        for i in range(3):
            b = h * 3 + i
            rows = pl.ds(b * BR, BR)
            lift = mm(low[pl.ds(b * RANK, RANK)], panel(usel, b), TN)
            base_rows = base[i * BR : (i + 1) * BR] + rs_right[3, rows].astype(F32) + rs_left[3, rows].astype(F32)
            kv[rows] = (live(b) * (base_rows + 0.5 * lift)).astype(BF16)
        store(kv.at[half[h]], kv_out.at[half[h]])

    for copy in sent.values():
        copy.wait_send()
    for copy in stores:
        copy.wait()


def local(tokens, frozen_weight, cotangent, down_maps, up_maps, stored_row, tenants, padding):
    shape = jax.ShapeDtypeStruct
    smem, anywhere = pl.BlockSpec(memory_space=pltpu.SMEM), pl.BlockSpec(memory_space=pl.ANY)
    vmem = pltpu.VMEM
    kv, gt, gd, gu = pl.pallas_call(
        kernel,
        name="projections",
        out_shape=(
            shape((ROWS, COLS), BF16), shape((ROWS, FEAT), BF16),
            shape((2, RANK, FEAT), BF16), shape((2, RANK, COLS), BF16),
        ),
        in_specs=[smem] * 3 + [anywhere] * 5,
        out_specs=[anywhere] * 4,
        scratch_shapes=[
            vmem((ROWS, FEAT), BF16),
            vmem((NZ, FEAT, COLS), BF16),
            vmem((NZ, ROWS, COLS), BF16),
            vmem((ROWS, FEAT), F32),
            vmem((4, ROWS, COLS), BF16),
            vmem((4, ROWS, COLS), BF16),
            vmem((4, HALF, COLS), BF16),
            vmem((ROWS, COLS), BF16),
            vmem((ROWS, FEAT), BF16),
            vmem((4, 4, 4, HR, FEAT), BF16),
            vmem((4, 4, 4, HR, COLS), BF16),
            vmem((2, NB, HR, FEAT), BF16),
            vmem((2, NB, HR, COLS), BF16),
            vmem((NB, HR, FEAT), BF16),
            vmem((NB, HR, COLS), BF16),
            vmem((4, 2, 8, 128), I32),
            pltpu.SMEM((4, 2, 8, 128), I32),
            pltpu.SMEM((16, 8), I32),
            vmem((NB * RANK, BR), BF16),
            vmem((NZ, 48, BR), BF16),
            vmem((NB * RANK, BR), BF16),
            vmem((NB * RANK, BR), BF16),
            vmem((NZ, 48, BR), BF16),
            vmem((NB * RANK, BR), BF16),
            vmem((2, NB, HR, FEAT), BF16),
            vmem((2, NB, HR, COLS), BF16),
            vmem((49, HR, FEAT), BF16),
            vmem((49, HR, COLS), BF16),
            vmem((4, 4, HR, FEAT), BF16),
            vmem((4, 4, HR, COLS), BF16),
            vmem((3, 4, HR, FEAT), BF16),
            vmem((3, 4, HR, COLS), BF16),
            vmem((4, HR, FEAT), BF16),
            vmem((4, HR, COLS), BF16),
            vmem((2, HR, FEAT), BF16),
            vmem((2, HR, COLS), BF16),
            pltpu.SemaphoreType.DMA((N_SEM,)),
            pltpu.SemaphoreType.DMA((N_SEM,)),
            pltpu.SemaphoreType.DMA((16,)),
            pltpu.SemaphoreType.DMA((8,)),
            pltpu.SemaphoreType.DMA((4,)),
        ],
        compiler_params=pltpu.CompilerParams(
            collective_id=0, has_side_effects=True, vmem_limit_bytes=56 * 2**20
        ),
    )(
        stored_row, tenants, padding, tokens, frozen_weight, cotangent,
        jnp.swapaxes(down_maps, 1, 2), up_maps,
    )
    return kv, gt, jnp.swapaxes(gd, 1, 2), gu


def solution(mesh):
    placed = (
        P("dp", "tensor"),
        P("tensor", None),
        P("dp", "tensor"),
        P("dp", "tensor", None),
        P("dp", None, "tensor"),
        P(),
        P("dp"),
        P("dp"),
    )
    return jax.shard_map(
        local,
        mesh=mesh,
        in_specs=placed,
        out_specs=(
            P("dp", "tensor"),
            P("dp", "tensor"),
            P("dp", "tensor", None),
            P("dp", None, "tensor"),
        ),
        check_vma=False,
    )
```

time: 304 us -> 107 us (0.35)
  waiting for transfers between devices: 183 us -> 0 us
  Pallas kernels: 0 us -> 100 us
  matrix products: 32.2 us -> 0 us
  starting transfers between devices: 27.2 us -> 0 us
  blocking collectives: 15.3 us -> 0 us
  local copies, waits for them, and re-layouts: 20.5 us -> 5.82 us
  between operations: 13.9 us -> 0.65 us
  other arithmetic: 9.57 us -> 0 us
    pallas_call x0 -> x1, Pallas kernels: none -> 100 us  [local(): pl.pallas_call(kernel, name='projections', out_shape=(shape((ROWS, COLS),...]
    all_to_all x4 -> x0, waiting for transfers between devices: 67.7 us -> none  [the longest x1 47.4 us: local(): lax.all_to_all(selected_down, 'dp', split_axis=0, concat_axis=0, tiled=True)]
    psum x1 -> x0, waiting for transfers between devices: 60.7 us -> none  [local(): low_rank = lax.psum(low_part.astype(jnp.bfloat16), 'tensor')]
    reduce_scatter x1 -> x0, waiting for transfers between devices: 39.3 us -> none  [local(): lax.psum_scatter(jnp.dot(tokens, frozen_weight, preferred_element_type=jn...]
    dot_general x10 -> x0, matrix products: 32.2 us -> none  [the longest x1 8.66 us: add_columns(): lax.dot_general(cot_piece, weight_rows, (((1,), (1,)), ((), ())), preferr...]
    all_to_all x4 -> x0, starting transfers between devices: 27.1 us -> none  [the longest x1 12.6 us: local(): lax.all_to_all(send_up, 'dp', split_axis=0, concat_axis=0, tiled=True)]
    all_to_all x1 -> x0, blocking collectives: 15.3 us -> none  [local(): lax.all_to_all(wanted[:, None], 'dp', split_axis=0, concat_axis=0, tiled=...]
    all_gather x1 -> x0, waiting for transfers between devices: 15.1 us -> none  [local(): lax.all_gather(flat_grad, 'tensor', axis=1, tiled=True)]
  transfers between devices with their start and end apart: 7 -> 0, of which waited for: 6 -> 0; matrix products, arithmetic and copies ran while one was open for 14% -> 0% of each run, Pallas kernels for 0% -> 0%
where the time goes in v1:
time: 107 us
  Pallas kernels  100 us (93%)
  local copies, waits for them, and re-layouts  5.82 us (5%)
    pallas_call x1, Pallas kernels, local(): pl.pallas_call(kernel, name='projections', out_shape=(shape((ROWS, COLS),...  100 us
    unnamed x8, local copies, waits for them, and re-layouts  5.82 us

profile of v1, /device:TPU:1, one launch (start us, length us, event | category | flops | bytes accessed | tf_op | source)
XLA Modules:
  0.0 106.8 jit_solution(12343561815341614169)
XLA Ops:
  0.6 100.3 %projections.1 = (bf16[768,256]{1,0:T(8,128)(2,1)}, bf16[768,1024]{1,0:T(8,128)(2,1)}, bf16[2,64,1024]{2,1,0:T(8,128)(2,1)}, bf16[2,64,256]{2,1,0:T(8,128)(2,1)}) custom-call(s32[64]{0:T(128)} %stored.1, s32[6]{0:T(128)} %tenants.1, s32[6]{0:T(128)} %padding.1, bf16[768,1024]{1,0:T(8,128)(2,1)} %tok_in.1, bf16[1024,2048]{1,0:T(8,128)(2,1)} %w_in.1, ...), custom_call_target="tpu_custom_call" | custom-call | tf_op jit(solution)/shard_map/projections/pallas_call | solution.py:456
  101.0 1.8 %copy.16 = bf16[768,256]{1,0:T(8,128)(2,1)} copy(bf16[768,256]{1,0:T(8,128)(2,1)} %get-tuple-element.16) | data formatting | bytes 786432
  102.7 0.0 copy-start
  102.7 0.0 copy-start.1
  102.7 2.7 %copy.17 = bf16[768,1024]{1,0:T(8,128)(2,1)} copy(bf16[768,1024]{1,0:T(8,128)(2,1)} %get-tuple-element.17) | data formatting | bytes 3145728
  105.5 0.0 copy-done
  105.5 0.7 copy.18
  106.2 0.0 copy-done.1
  106.2 0.6 copy.19
Async XLA Ops:
  102.7 2.7 %copy-start = (bf16[2,64,1024]{2,1,0:T(8,128)(2,1)S(1)}, bf16[2,64,1024]{2,1,0:T(8,128)(2,1)}, u32[]{:S(2)}) copy-start(bf16[2,64,1024]{2,1,0:T(8,128)(2,1)} %get-tuple-element.10) | copy-start | bytes 786436
  102.7 3.4 %copy-start.1 = (bf16[2,64,256]{2,1,0:T(8,128)(2,1)S(1)}, bf16[2,64,256]{2,1,0:T(8,128)(2,1)}, u32[]{:S(2)}) copy-start(bf16[2,64,256]{2,1,0:T(8,128)(2,1)} %get-tuple-element.19) | copy-start | bytes 196612

commit v2 on v0

v2 whole, which is shorter than its diff:
```python
import jax
import jax.numpy as jnp
from jax import lax
from jax.experimental import pallas as pl
from jax.experimental.pallas import tpu as pltpu
from jax.sharding import PartitionSpec as P

MESH = pl.DeviceIdType.MESH
F32, BF16, I32 = jnp.float32, jnp.bfloat16, jnp.int32
NT = (((1,), (1,)), ((), ()))
TN = (((0,), (0,)), ((), ()))
NZ, NB, BR = 8, 6, 128
ROWS, HALF = 768, 384
FEAT, COLS, RANK, HR = 1024, 256, 64, 32
N_SEM = 160


def mm(a, b, dims=None):
    if dims is None:
        return jnp.dot(a, b, preferred_element_type=F32)
    return lax.dot_general(a, b, dims, preferred_element_type=F32)


def kernel(
    stored, tenants, padding, tok_in, w_in, cot_in, down_in, up_in,
    kv, gt, gd, gu,
    tok, w, g, g_sib, acc, kv_acc, rs_right, rs_left, rs_first,
    ad, au, dh, uh, dx, ux, ints, ints_smem, table,
    low_part, low_recv, low, low_x, back_part, back_recv, back, back_x,
    rd, ru, qd, qu, qd_in, qu_in,
    send_sem, recv_sem, load_sem, copy_sem,
):
    dp, z = lax.axis_index("dp"), lax.axis_index("tensor")
    y, x, c = dp // 8, (dp // 2) % 4, dp % 2
    mp, mq = (1 - c) * x + c * y, (1 - c) * y + c * x

    def z_at(step):
        return (dp, (z + step + NZ) % NZ)

    def chip_at(dy, dx_, core):
        return (((y + dy + 4) % 4) * 8 + ((x + dx_ + 4) % 4) * 2 + core, z)

    def p_at(step):
        return chip_at(c * step, (1 - c) * step, c)

    def q_at(step):
        return chip_at((1 - c) * step, c * step, c)

    def p_cross(step):
        return chip_at(c * step, (1 - c) * step, 1 - c)

    def q_cross(step):
        return chip_at((1 - c) * step, c * step, 1 - c)

    sibling = (dp + 1 - 2 * c, z)
    sent = {}

    def send(key, src, dst, device):
        n = len(sent)
        copy = pltpu.make_async_remote_copy(
            src_ref=src, dst_ref=dst, send_sem=send_sem.at[n], recv_sem=recv_sem.at[n],
            device_id=device, device_id_type=MESH,
        )
        copy.start()
        sent[key] = copy

    arrived = set()

    def recv(key):
        if key not in arrived:
            arrived.add(key)
            sent[key].wait_recv()

    loads = {}

    def load(key, src, dst):
        loads[key] = pltpu.make_async_copy(src, dst, load_sem.at[len(loads)])
        loads[key].start()

    mine, others = pl.ds(c * HR, HR), pl.ds((1 - c) * HR, HR)
    load("g", cot_in, g.at[0])
    load("u", up_in.at[:, mine], au.at[0, 0, 0])
    load("d", down_in.at[:, mine], ad.at[0, 0, 0])
    load("tok", tok_in, tok.at[0])
    for k in (4, 3, 5, 0, 2, 6, 1, 7):
        load(("w", k), w_in.at[:, pl.ds(((z + k) % NZ) * COLS, COLS)], w.at[k])

    barrier = pltpu.get_barrier_semaphore()
    friends = [z_at(k) for k in range(1, NZ)] + [p_at(1), p_at(-1), q_at(1), q_at(-1), sibling]
    friends += [q_cross(1), q_cross(-1)]
    for friend in friends:
        pl.semaphore_signal(barrier, inc=1, device_id=friend, device_id_type=MESH)

    lane = lax.broadcasted_iota(I32, (8, 128), 1)
    tile = jnp.zeros((8, 128), I32)
    for b in range(NB):
        tile = jnp.where(lane == b, stored[tenants[b]], tile)
    ints[0, 0] = tile

    position = lax.broadcasted_iota(I32, (BR, 1), 0)

    def live(b):
        return (position < BR - padding[b]).astype(F32)

    loads["g"].wait()
    for b in range(NB):
        rows = pl.ds(b * BR, BR)
        g[0, rows] = (g[0, rows].astype(F32) * live(b)).astype(BF16)

    pl.semaphore_wait(barrier, len(friends))

    half = (pl.ds(0, HALF), pl.ds(HALF, HALF))

    def ag_send(step, h, right):
        src, dst = ((-step) % NZ, (-step - 1) % NZ) if right else (step, step + 1)
        send(("ag", right, step, h), g.at[src, half[h]], g.at[dst, half[h]], z_at(1 if right else -1))

    def ag_pass(step, h):
        for right in (True, False):
            recv(("ag", right, step, h))
            if step < 2 or (h == 0) == right:
                ag_send(step + 1, h, right)

    def partial(k, h):
        return mm(tok[0, half[h]], w[k])

    def rs_start(step, h, right):
        k = (4 - step) if right else (4 + step)
        slot = step * 2 + (0 if right else 1)
        rs_first[slot] = partial(k, h).astype(BF16)
        dst = rs_right if right else rs_left
        send(("rs", right, step, h), rs_first.at[slot], dst.at[step, half[h]], z_at(1 if right else -1))

    def rs_pass(step, h):
        for right in (True, False):
            if step == 1 and (h == 0) != right:
                continue
            k = (4 - step) if right else (4 + step)
            buf = rs_right if right else rs_left
            own = partial(k, h)
            recv(("rs", right, step - 1, h))
            buf[step - 1, half[h]] = (buf[step - 1, half[h]].astype(F32) + own).astype(BF16)
            send(("rs", right, step, h), buf.at[step - 1, half[h]], buf.at[step, half[h]], z_at(1 if right else -1))

    def f1_send(name, a, r):
        send((name, "f1", 1, r), a.at[0, 0, r], a.at[0, 3, r], p_at(1))
        send((name, "f1", -1, r), a.at[0, 0, r], a.at[0, 1, r], p_at(-1))

    def f1_pass(name, a):
        recv((name, "f1", 1, 0))
        send((name, "f1x", 1), a.at[0, 3, 0], a.at[0, 2, 0], p_at(1))
        recv((name, "f1", -1, 1))
        send((name, "f1x", -1), a.at[0, 1, 1], a.at[0, 2, 1], p_at(-1))
        recv((name, "f1", 1, 1))
        recv((name, "f1", -1, 0))

    def f1_end(name):
        recv((name, "f1x", 1))
        recv((name, "f1x", -1))

    def f2_send(name, a, rp):
        send((name, "f2", 1, rp), a.at[0, rp], a.at[3, rp], q_at(1))
        send((name, "f2", -1, rp), a.at[0, rp], a.at[1, rp], q_at(-1))

    def f2_pass(name, a, rp):
        recv((name, "f2", 1, rp))
        send((name, "f2x", 1, rp), a.at[3, rp, 0], a.at[2, rp, 0], q_at(1))
        recv((name, "f2", -1, rp))
        send((name, "f2x", -1, rp), a.at[1, rp, 1], a.at[2, rp, 1], q_at(-1))

    def f2_end(name):
        for rp in range(4):
            recv((name, "f2x", 1, rp))
            recv((name, "f2x", -1, rp))

    def fetch_0(name, a):
        recv((name, "f0"))
        f1_send(name, a, 1)
        f2_send(name, a, 0)

    def fetch_1(name, a):
        f1_pass(name, a)
        f2_send(name, a, 3)
        f2_send(name, a, 1)

    def fetch_2(name, a):
        f1_end(name)
        f2_send(name, a, 2)

    def fetch_3(name, a):
        f2_pass(name, a, 0)

    def fetch_4(name, a):
        f2_pass(name, a, 3)
        f2_pass(name, a, 1)

    def fetch_5(name, a):
        f2_pass(name, a, 2)

    def place(slot):
        chip, inner = slot // 4, slot % 4
        cy, cx = chip // 4, chip % 4
        rq = ((1 - c) * cy + c * cx - mq + 4) % 4
        rp = ((1 - c) * cx + c * cy - mp + 4) % 4
        return rq, rp, (inner // 2 + c) % 2, inner % 2

    def pick(name, a, picked, out):
        f2_end(name)
        for r in (1, 0):
            for b in range(NB):
                rq, rp, core, inner = place(ints_smem[0, r, 0, b])
                picked[r, b] = a[rq, rp, core, inner]
        send((name, "pick"), picked.at[1], out, sibling)

    def sum_scatter(name, part, got):
        for k in range(1, NZ):
            rows = pl.ds(((z + k) % NZ) * 48, 48)
            send((name, "s", k), part.at[rows], got.at[k], z_at(k))

    def sum_gather(name, part, got, total, scale):
        own = pl.ds(z * 48, 48)
        value = part[own].astype(F32)
        for k in range(1, NZ):
            recv((name, "s", k))
            value = value + got[k].astype(F32)
        total[own] = (value * scale).astype(BF16)
        for k in range(1, NZ):
            send((name, "g", k), total.at[own], total.at[own], z_at(k))

    def sum_end(name, total, out):
        for k in range(1, NZ):
            recv((name, "g", k))
        send((name, "x"), total.at[pl.ds(NB * HR, NB * HR)], out, sibling)

    def rank_rows(r, b):
        return pl.ds((r * NB + b) * HR, HR)

    def block(b):
        return pl.ds(b * BR, BR)

    def back_begin():
        pick("u", au, uh, ux)
        recv("xg")
        for b in range(NB):
            back_part[rank_rows(0, b)] = mm(uh[0, b], g[0, block(b)], NT).astype(BF16)
            back_part[rank_rows(1, b)] = mm(uh[1, b], g_sib[block(b)], NT).astype(BF16)
        sum_scatter("back", back_part, back_recv)

    def low_begin():
        pick("d", ad, dh, dx)
        recv("xtok")
        for r in (0, 1):
            for b in range(NB):
                low_part[rank_rows(r, b)] = mm(dh[r, b], tok[r, block(b)], NT).astype(BF16)
        sum_scatter("low", low_part, low_recv)

    def terms_send(name, r, core):
        src = r.at[pl.ds(core * NB, NB)]
        send((name, "t1", 1, core), src, r.at[pl.ds(36 + core * NB, NB)], q_at(1))
        send((name, "t1", -1, core), src, r.at[pl.ds(12 + core * NB, NB)], q_at(-1))

    def down_terms():
        sum_end("back", back, back_x)
        recv("xtok")
        for r in (0, 1):
            for b in range(NB):
                rd[r * NB + b] = mm(back[rank_rows(r, b)], tok[r, block(b)]).astype(BF16)
            terms_send("d", rd, r)

    def up_terms():
        sum_end("low", low, low_x)
        for b in range(NB):
            ru[b] = (0.5 * mm(low[rank_rows(0, b)], g[0, block(b)])).astype(BF16)
        terms_send("u", ru, 0)
        for b in range(NB):
            ru[NB + b] = (0.5 * mm(low[rank_rows(1, b)], g_sib[block(b)])).astype(BF16)
        terms_send("u", ru, 1)

    def terms_pass(name, r):
        recv((name, "t1", 1, 0))
        send((name, "t2", 1), r.at[pl.ds(36, NB)], r.at[pl.ds(24, NB)], q_at(1))
        recv((name, "t1", -1, 1))
        send((name, "t2", -1), r.at[pl.ds(12 + NB, NB)], r.at[pl.ds(24 + NB, NB)], q_at(-1))
        recv((name, "t1", 1, 1))
        recv((name, "t1", -1, 0))

    def fill_table():
        rd[48] = jnp.zeros((HR, FEAT), BF16)
        ru[48] = jnp.zeros((HR, COLS), BF16)

        def body(j, _):
            pj, core = (mp + j // 4) % 4, (j // 2 + c) % 2
            slot = (((1 - c) * mq + c * pj) * 4 + (1 - c) * pj + c * mq) * 4 + core * 2 + j % 2
            for i in range(4):
                for r in range(2):
                    entry = I32(48)
                    for b in range(NB):
                        entry = jnp.where(ints_smem[i, r, 0, b] == slot, (i * 2 + r) * NB + b, entry)
                    table[j, i * 2 + r] = entry
            return 0

        lax.fori_loop(0, 16, body, 0)

    def add_up(r, q, j):
        def body(inner, _):
            total = r[table[j * 4 + inner, 0]].astype(F32)
            for d in range(1, 8):
                total = total + r[table[j * 4 + inner, d]].astype(F32)
            q[j, inner // 2, inner % 2] = total.astype(BF16)
            return 0

        lax.fori_loop(0, 4, body, 0)

    def sums_send(name, r, q, q_in):
        recv((name, "t2", 1))
        recv((name, "t2", -1))
        add_up(r, q, 2)
        send((name, "q0", 1), q.at[2, 0], q_in.at[5], p_at(1))
        send((name, "q0", -1), q.at[2, 1], q_in.at[6], p_at(-1))
        add_up(r, q, 1)
        send((name, "q2", 1), q.at[1, 1], q_in.at[2], p_cross(1))
        add_up(r, q, 3)
        send((name, "q1", -1), q.at[3, 0], q_in.at[1], p_at(-1))
        add_up(r, q, 0)
        send((name, "q3"), q.at[0, 1], q_in.at[4], sibling)

    def sums_pass(name, q, q_in):
        recv((name, "q0", 1))
        q[1, 0] = (q[1, 0].astype(F32) + q_in[5].astype(F32)).astype(BF16)
        send((name, "q1", 1), q.at[1, 0], q_in.at[0], p_at(1))
        recv((name, "q0", -1))
        q[3, 1] = (q[3, 1].astype(F32) + q_in[6].astype(F32)).astype(BF16)
        send((name, "q2", -1), q.at[3, 1], q_in.at[3], p_cross(-1))

    def sums_end(name, q, q_in, out):
        recv((name, "q1", 1))
        recv((name, "q1", -1))
        recv((name, "q2", 1))
        recv((name, "q2", -1))
        recv((name, "q3"))
        for k in range(2):
            out[k, mine] = (q[0, 0, k].astype(F32) + q_in[0, k].astype(F32) + q_in[1, k].astype(F32)).astype(BF16)
            out[k, others] = (
                q_in[2, k].astype(F32) + q_in[3, k].astype(F32) + q_in[4, k].astype(F32)
            ).astype(BF16)

    def acc_first():
        loads[("w", 0)].wait()

        def body(i, _):
            rows = pl.ds(i * 256, 256)
            acc[rows] = mm(g[0, rows], w[0], NT)
            return 0

        lax.fori_loop(0, 3, body, 0)

    def acc_pair(k):
        def body(i, _):
            rows = pl.ds(i * 256, 256)
            acc[rows] += mm(g[k, rows], w[k], NT) + mm(g[NZ - k, rows], w[NZ - k], NT)
            return 0

        lax.fori_loop(0, 3, body, 0)

    def both(a, b):
        return jnp.concatenate([a, b], axis=0)

    def side():
        recv(("back", "x"))
        recv(("d", "pick"))
        for b in range(NB):
            rows = block(b)
            panel, inner = both(dh[0, b], dx[b]), both(back[rank_rows(0, b)], back_x[rank_rows(0, b)])
            acc[rows] += mm(inner, panel, TN)

    def last_gather():
        recv(("ag", True, 3, 0))
        recv(("ag", False, 3, 1))

        def body(i, _):
            rows = pl.ds(i * 256, 256)
            gt[rows] = (acc[rows] + mm(g[4, rows], w[4], NT)).astype(BF16)
            return 0

        lax.fori_loop(0, 3, body, 0)

    def lift():
        recv(("low", "x"))
        recv(("u", "pick"))
        for b in range(NB):
            panel, inner = both(uh[0, b], ux[b]), both(low[rank_rows(0, b)], low_x[rank_rows(0, b)])
            rows = block(b)
            kv_acc[rows] = mm(tok[0, rows], w[0]) + 0.5 * mm(inner, panel, TN)

    def last_sum():
        for h in (0, 1):
            recv(("rs", True, 3, h))
            recv(("rs", False, 3, h))
            for b in range(h * 3, h * 3 + 3):
                rows = block(b)
                total = kv_acc[rows] + rs_right[3, rows].astype(F32) + rs_left[3, rows].astype(F32)
                kv[rows] = (live(b) * total).astype(BF16)

    def start():
        for h in (0, 1):
            ag_send(0, h, True)
            ag_send(0, h, False)
        send(("u", "f0"), up_in.at[:, others], au.at[0, 0, 1], sibling)
        send("f0i", ints.at[0, 0], ints.at[0, 1], sibling)
        loads["u"].wait()
        f1_send("u", au, 0)
        send(("d", "f0"), down_in.at[:, others], ad.at[0, 0, 1], sibling)
        loads["d"].wait()
        f1_send("d", ad, 0)
        send("xg", g.at[0], g_sib, sibling)

    def rs_begin():
        loads["tok"].wait()
        loads[("w", 4)].wait()
        rs_start(0, 0, True)
        rs_start(0, 1, False)
        loads[("w", 3)].wait()
        rs_start(1, 1, True)
        loads[("w", 5)].wait()
        rs_start(1, 0, False)
        send("xtok", tok.at[0], tok.at[1], sibling)
        for k in (2, 6, 1, 7):
            loads[("w", k)].wait()

    def ints_0():
        recv("f0i")
        send(("i", 1), ints.at[0], ints.at[3], q_at(1))
        send(("i", -1), ints.at[0], ints.at[1], q_at(-1))

    def ints_1():
        recv(("i", 1))
        send(("i", 2), ints.at[3], ints.at[2], q_at(1))

    def ints_2():
        recv(("i", -1))
        recv(("i", 2))
        to_smem = pltpu.make_async_copy(ints, ints_smem, copy_sem)
        to_smem.start()
        to_smem.wait()

    start()
    fetch_0("u", au)
    fetch_0("d", ad)
    fetch_1("u", au)
    fetch_3("u", au)
    ints_0()
    fetch_2("u", au)
    rs_begin()
    ag_pass(0, 1)
    fetch_1("d", ad)
    fetch_5("u", au)
    fetch_4("u", au)
    ints_1()
    ints_2()
    back_begin()
    fetch_4("d", ad)
    fill_table()
    ag_pass(0, 0)
    fetch_2("d", ad)
    fetch_5("d", ad)
    fetch_3("d", ad)
    ag_pass(1, 1)
    acc_first()
    sum_gather("back", back_part, back_recv, back, 0.5)
    low_begin()
    ag_pass(1, 0)
    down_terms()
    rs_pass(1, 1)
    rs_pass(1, 0)
    sum_gather("low", low_part, low_recv, low, 1.0)
    terms_pass("d", rd)
    rs_pass(2, 1)
    ag_pass(2, 1)
    ag_pass(2, 0)
    up_terms()
    acc_pair(1)
    acc_pair(2)
    rs_pass(2, 0)
    sums_send("d", rd, qd, qd_in)
    side()
    rs_pass(3, 1)
    terms_pass("u", ru)
    acc_pair(3)
    rs_pass(3, 0)
    sums_pass("d", qd, qd_in)
    last_gather()
    sums_send("u", ru, qu, qu_in)
    sums_pass("u", qu, qu_in)
    lift()
    sums_end("d", qd, qd_in, gd)
    sums_end("u", qu, qu_in, gu)
    last_sum()

    for copy in sent.values():
        copy.wait_send()


def local(tokens, frozen_weight, cotangent, down_maps, up_maps, stored_row, tenants, padding):
    shape = jax.ShapeDtypeStruct
    smem, anywhere = pl.BlockSpec(memory_space=pltpu.SMEM), pl.BlockSpec(memory_space=pl.ANY)
    vmem = pltpu.VMEM
    inside = pl.BlockSpec(memory_space=vmem)
    shapes = (
        shape((ROWS, COLS), BF16), shape((ROWS, FEAT), BF16),
        shape((2, RANK, FEAT), BF16), shape((2, RANK, COLS), BF16),
    )
    kv, gt, gd, gu = pl.pallas_call(
        kernel,
        name="projections",
        out_shape=tuple(vmem(s.shape, s.dtype) for s in shapes),
        in_specs=[smem] * 3 + [pl.BlockSpec(memory_space=pltpu.HBM)] * 5,
        out_specs=[inside] * 4,
        scratch_shapes=[
            vmem((2, ROWS, FEAT), BF16),
            vmem((NZ, FEAT, COLS), BF16),
            vmem((NZ, ROWS, COLS), BF16),
            vmem((ROWS, COLS), BF16),
            vmem((ROWS, FEAT), F32),
            vmem((ROWS, COLS), F32),
            vmem((4, ROWS, COLS), BF16),
            vmem((4, ROWS, COLS), BF16),
            vmem((4, HALF, COLS), BF16),
            vmem((4, 4, 2, 2, HR, FEAT), BF16),
            vmem((4, 4, 2, 2, HR, COLS), BF16),
            vmem((2, NB, HR, FEAT), BF16),
            vmem((2, NB, HR, COLS), BF16),
            vmem((NB, HR, FEAT), BF16),
            vmem((NB, HR, COLS), BF16),
            vmem((4, 2, 8, 128), I32),
            pltpu.SMEM((4, 2, 8, 128), I32),
            pltpu.SMEM((16, 8), I32),
            vmem((2 * NB * HR, BR), BF16),
            vmem((NZ, 48, BR), BF16),
            vmem((2 * NB * HR, BR), BF16),
            vmem((NB * HR, BR), BF16),
            vmem((2 * NB * HR, BR), BF16),
            vmem((NZ, 48, BR), BF16),
            vmem((2 * NB * HR, BR), BF16),
            vmem((NB * HR, BR), BF16),
            vmem((49, HR, FEAT), BF16),
            vmem((49, HR, COLS), BF16),
            vmem((4, 2, 2, HR, FEAT), BF16),
            vmem((4, 2, 2, HR, COLS), BF16),
            vmem((7, 2, HR, FEAT), BF16),
            vmem((7, 2, HR, COLS), BF16),
            pltpu.SemaphoreType.DMA((N_SEM,)),
            pltpu.SemaphoreType.DMA((N_SEM,)),
            pltpu.SemaphoreType.DMA((16,)),
            pltpu.SemaphoreType.DMA,
        ],
        compiler_params=pltpu.CompilerParams(
            collective_id=0, has_side_effects=True, vmem_limit_bytes=60 * 2**20
        ),
    )(
        stored_row, tenants, padding, tokens, frozen_weight, cotangent,
        jnp.swapaxes(down_maps, 1, 2), up_maps,
    )
    return kv, gt, jnp.swapaxes(gd, 1, 2), gu


def solution(mesh):
    placed = (
        P("dp", "tensor"),
        P("tensor", None),
        P("dp", "tensor"),
        P("dp", "tensor", None),
        P("dp", None, "tensor"),
        P(),
        P("dp"),
        P("dp"),
    )
    return jax.shard_map(
        local,
        mesh=mesh,
        in_specs=placed,
        out_specs=(
            P("dp", "tensor"),
            P("dp", "tensor"),
            P("dp", "tensor", None),
            P("dp", None, "tensor"),
        ),
        check_vma=False,
    )
```

time: 304 us -> 95.4 us (0.31)
  waiting for transfers between devices: 183 us -> 0 us
  Pallas kernels: 0 us -> 91.4 us
  matrix products: 32.2 us -> 0 us
  starting transfers between devices: 27.2 us -> 0 us
  local copies, waits for them, and re-layouts: 20.5 us -> 3.22 us
  blocking collectives: 15.3 us -> 0 us
  between operations: 13.9 us -> 0.64 us
  other arithmetic: 9.57 us -> 0 us
    pallas_call x0 -> x1, Pallas kernels: none -> 91.4 us  [local(): pl.pallas_call(kernel, name='projections', out_shape=tuple((vmem(s.shape,...]
    all_to_all x4 -> x0, waiting for transfers between devices: 67.7 us -> none  [the longest x1 47.4 us: local(): lax.all_to_all(selected_down, 'dp', split_axis=0, concat_axis=0, tiled=True)]
    psum x1 -> x0, waiting for transfers between devices: 60.7 us -> none  [local(): low_rank = lax.psum(low_part.astype(jnp.bfloat16), 'tensor')]
    reduce_scatter x1 -> x0, waiting for transfers between devices: 39.3 us -> none  [local(): lax.psum_scatter(jnp.dot(tokens, frozen_weight, preferred_element_type=jn...]
    dot_general x10 -> x0, matrix products: 32.2 us -> none  [the longest x1 8.66 us: add_columns(): lax.dot_general(cot_piece, weight_rows, (((1,), (1,)), ((), ())), preferr...]
    all_to_all x4 -> x0, starting transfers between devices: 27.1 us -> none  [the longest x1 12.6 us: local(): lax.all_to_all(send_up, 'dp', split_axis=0, concat_axis=0, tiled=True)]
    all_to_all x1 -> x0, blocking collectives: 15.3 us -> none  [local(): lax.all_to_all(wanted[:, None], 'dp', split_axis=0, concat_axis=0, tiled=...]
    all_gather x1 -> x0, waiting for transfers between devices: 15.1 us -> none  [local(): lax.all_gather(flat_grad, 'tensor', axis=1, tiled=True)]
  transfers between devices with their start and end apart: 7 -> 0, of which waited for: 6 -> 0; matrix products, arithmetic and copies ran while one was open for 14% -> 0% of each run, Pallas kernels for 0% -> 0%
where the time goes in v2:
time: 95.4 us; the launch traced here: 95.3 us
  Pallas kernels  91.4 us (96%)
  local copies, waits for them, and re-layouts  3.22 us (3%)
    pallas_call x1, Pallas kernels, local(): pl.pallas_call(kernel, name='projections', out_shape=tuple((vmem(s.shape,...  91.4 us
    unnamed x4, local copies, waits for them, and re-layouts  3.22 us

profile of v2, /device:TPU:1, one launch (start us, length us, event | category | flops | bytes accessed | tf_op | source)
XLA Modules:
  0.0 95.3 jit_solution(11833340214033702368)
XLA Ops:
  0.6 91.4 %projections.1 = (bf16[768,256]{1,0:T(8,128)(2,1)S(1)}, bf16[768,1024]{1,0:T(8,128)(2,1)S(1)}, bf16[2,64,1024]{2,1,0:T(8,128)(2,1)S(1)}, bf16[2,64,256]{2,1,0:T(8,128)(2,1)S(1)}) custom-call(s32[64]{0:T(128)} %stored.1, s32[6]{0:T(128)} %tenants.1, s32[6]{0:T(128)} %padding.1, bf16[768,1024]{1,0:T(8,128)(2,1)} %tok_in.1, bf16[1024,2048]{1,0:T(8,128)(2,1)} %w_in.1, ...), custom_call_target="tpu_custom_call" | custom-call | tf_op jit(solution)/shard_map/projections/pallas_call | solution.py:512
  92.1 0.7 copy.16
  92.8 0.6 copy.19
  93.4 0.7 copy.18
  94.1 1.1 %copy.17 = bf16[768,1024]{1,0:T(8,128)(2,1)} copy(bf16[768,1024]{1,0:T(8,128)(2,1)S(1)} %get-tuple-element.13) | data formatting | bytes 3145728

commit v3 on v2

--- a/solution.py
+++ b/solution.py
@@ -10,9 +10,9 @@
 NT = (((1,), (1,)), ((), ()))
 TN = (((0,), (0,)), ((), ()))
 NZ, NB, BR = 8, 6, 128
-ROWS, HALF = 768, 384
+ROWS, PIECES, PIECE = 768, 4, 192
 FEAT, COLS, RANK, HR = 1024, 256, 64, 32
-N_SEM = 160
+N_SEM = 200
 
 
 def mm(a, b, dims=None):
@@ -77,6 +77,16 @@
         loads[key] = pltpu.make_async_copy(src, dst, load_sem.at[len(loads)])
         loads[key].start()
 
+    loaded = set()
+
+    def wait_load(key):
+        if key not in loaded:
+            loaded.add(key)
+            loads[key].wait()
+
+    def wait_w(k):
+        wait_load(("w", k))
+
     mine, others = pl.ds(c * HR, HR), pl.ds((1 - c) * HR, HR)
     load("g", cot_in, g.at[0])
     load("u", up_in.at[:, mine], au.at[0, 0, 0])
@@ -102,14 +112,17 @@
     def live(b):
         return (position < BR - padding[b]).astype(F32)
 
-    loads["g"].wait()
+    wait_load("g")
     for b in range(NB):
         rows = pl.ds(b * BR, BR)
         g[0, rows] = (g[0, rows].astype(F32) * live(b)).astype(BF16)
 
     pl.semaphore_wait(barrier, len(friends))
 
-    half = (pl.ds(0, HALF), pl.ds(HALF, HALF))
+    half = [pl.ds(h * PIECE, PIECE) for h in range(PIECES)]
+
+    def goes_right(h):
+        return h < PIECES // 2
 
     def ag_send(step, h, right):
         src, dst = ((-step) % NZ, (-step - 1) % NZ) if right else (step, step + 1)
@@ -118,22 +131,28 @@
     def ag_pass(step, h):
         for right in (True, False):
             recv(("ag", right, step, h))
-            if step < 2 or (h == 0) == right:
+            if step < 2 or goes_right(h) == right:
                 ag_send(step + 1, h, right)
 
     def partial(k, h):
         return mm(tok[0, half[h]], w[k])
 
-    def rs_start(step, h, right):
-        k = (4 - step) if right else (4 + step)
-        slot = step * 2 + (0 if right else 1)
-        rs_first[slot] = partial(k, h).astype(BF16)
-        dst = rs_right if right else rs_left
-        send(("rs", right, step, h), rs_first.at[slot], dst.at[step, half[h]], z_at(1 if right else -1))
+    def rs_start(h):
+        wait_load("tok")
+        for right in (True, False):
+            step = 0 if goes_right(h) == right else 1
+            k = (4 - step) if right else (4 + step)
+            wait_w(k)
+            slot = 0 if right else 1
+            rs_first[slot, half[h]] = partial(k, h).astype(BF16)
+            dst = rs_right if right else rs_left
+            send(("rs", right, step, h), rs_first.at[slot, half[h]], dst.at[step, half[h]], z_at(1 if right else -1))
 
     def rs_pass(step, h):
+        wait_w(4 - step)
+        wait_w(4 + step)
         for right in (True, False):
-            if step == 1 and (h == 0) != right:
+            if step == 1 and goes_right(h) != right:
                 continue
             k = (4 - step) if right else (4 + step)
             buf = rs_right if right else rs_left
@@ -345,7 +364,7 @@
             ).astype(BF16)
 
     def acc_first():
-        loads[("w", 0)].wait()
+        wait_w(0)
 
         def body(i, _):
             rows = pl.ds(i * 256, 256)
@@ -355,6 +374,9 @@
         lax.fori_loop(0, 3, body, 0)
 
     def acc_pair(k):
+        wait_w(k)
+        wait_w(NZ - k)
+
         def body(i, _):
             rows = pl.ds(i * 256, 256)
             acc[rows] += mm(g[k, rows], w[k], NT) + mm(g[NZ - k, rows], w[NZ - k], NT)
@@ -374,8 +396,9 @@
             acc[rows] += mm(inner, panel, TN)
 
     def last_gather():
-        recv(("ag", True, 3, 0))
-        recv(("ag", False, 3, 1))
+        wait_w(4)
+        for h in range(PIECES):
+            recv(("ag", goes_right(h), 3, h))
 
         def body(i, _):
             rows = pl.ds(i * 256, 256)
@@ -385,6 +408,8 @@
         lax.fori_loop(0, 3, body, 0)
 
     def lift():
+        wait_w(0)
+        wait_load("tok")
         recv(("low", "x"))
         recv(("u", "pick"))
         for b in range(NB):
@@ -393,39 +418,37 @@
             kv_acc[rows] = mm(tok[0, rows], w[0]) + 0.5 * mm(inner, panel, TN)
 
     def last_sum():
-        for h in (0, 1):
+        done = 0
+        for h in range(PIECES):
             recv(("rs", True, 3, h))
             recv(("rs", False, 3, h))
-            for b in range(h * 3, h * 3 + 3):
+            for b in range(done, (h + 1) * NB // PIECES):
                 rows = block(b)
                 total = kv_acc[rows] + rs_right[3, rows].astype(F32) + rs_left[3, rows].astype(F32)
                 kv[rows] = (live(b) * total).astype(BF16)
-
-    def start():
-        for h in (0, 1):
-            ag_send(0, h, True)
-            ag_send(0, h, False)
+            done = (h + 1) * NB // PIECES
+
+    def ag_start(h):
+        ag_send(0, h, True)
+        ag_send(0, h, False)
+
+    def up_start():
         send(("u", "f0"), up_in.at[:, others], au.at[0, 0, 1], sibling)
         send("f0i", ints.at[0, 0], ints.at[0, 1], sibling)
-        loads["u"].wait()
+        wait_load("u")
         f1_send("u", au, 0)
+
+    def down_start():
         send(("d", "f0"), down_in.at[:, others], ad.at[0, 0, 1], sibling)
-        loads["d"].wait()
+        wait_load("d")
         f1_send("d", ad, 0)
+
+    def grad_rows_out():
         send("xg", g.at[0], g_sib, sibling)
 
-    def rs_begin():
-        loads["tok"].wait()
-        loads[("w", 4)].wait()
-        rs_start(0, 0, True)
-        rs_start(0, 1, False)
-        loads[("w", 3)].wait()
-        rs_start(1, 1, True)
-        loads[("w", 5)].wait()
-        rs_start(1, 0, False)
+    def tokens_out():
+        wait_load("tok")
         send("xtok", tok.at[0], tok.at[1], sibling)
-        for k in (2, 6, 1, 7):
-            loads[("w", k)].wait()
 
     def ints_0():
         recv("f0i")
@@ -443,57 +466,79 @@
         to_smem.start()
         to_smem.wait()
 
-    start()
+    ag_start(2)
+    ag_start(3)
+    up_start()
     fetch_0("u", au)
-    fetch_0("d", ad)
+    down_start()
+    ints_0()
+    rs_start(2)
+    ag_start(1)
     fetch_1("u", au)
     fetch_3("u", au)
-    ints_0()
     fetch_2("u", au)
-    rs_begin()
-    ag_pass(0, 1)
+    ag_start(0)
+    grad_rows_out()
+    rs_start(0)
+    fetch_0("d", ad)
+    ints_1()
+    ag_pass(0, 3)
+    fetch_4("u", au)
+    rs_start(1)
+    rs_start(3)
+    tokens_out()
+    acc_first()
+    rs_pass(1, 2)
+    fetch_5("u", au)
     fetch_1("d", ad)
-    fetch_5("u", au)
-    fetch_4("u", au)
-    ints_1()
     ints_2()
     back_begin()
-    fetch_4("d", ad)
-    fill_table()
-    ag_pass(0, 0)
-    fetch_2("d", ad)
-    fetch_5("d", ad)
+    ag_pass(0, 1)
     fetch_3("d", ad)
-    ag_pass(1, 1)
-    acc_first()
-    sum_gather("back", back_part, back_recv, back, 0.5)
-    low_begin()
-    ag_pass(1, 0)
-    down_terms()
     rs_pass(1, 1)
     rs_pass(1, 0)
+    fetch_2("d", ad)
+    fetch_4("d", ad)
+    rs_pass(1, 3)
+    sum_gather("back", back_part, back_recv, back, 0.5)
+    ag_pass(0, 2)
+    ag_pass(0, 0)
+    rs_pass(2, 2)
+    fetch_5("d", ad)
+    rs_pass(2, 1)
+    low_begin()
+    down_terms()
+    ag_pass(1, 2)
+    fill_table()
+    ag_pass(1, 0)
+    side()
     sum_gather("low", low_part, low_recv, low, 1.0)
+    rs_pass(3, 2)
+    rs_pass(2, 3)
     terms_pass("d", rd)
-    rs_pass(2, 1)
+    ag_pass(1, 1)
+    acc_pair(1)
+    ag_pass(1, 3)
+    acc_pair(2)
+    up_terms()
+    rs_pass(2, 0)
+    ag_pass(2, 0)
+    sums_send("d", rd, qd, qd_in)
+    terms_pass("u", ru)
+    ag_pass(2, 3)
+    ag_pass(2, 2)
+    rs_pass(3, 1)
+    sums_pass("d", qd, qd_in)
     ag_pass(2, 1)
-    ag_pass(2, 0)
-    up_terms()
-    acc_pair(1)
-    acc_pair(2)
-    rs_pass(2, 0)
-    sums_send("d", rd, qd, qd_in)
-    side()
-    rs_pass(3, 1)
-    terms_pass("u", ru)
     acc_pair(3)
+    sums_send("u", ru, qu, qu_in)
     rs_pass(3, 0)
-    sums_pass("d", qd, qd_in)
+    rs_pass(3, 3)
+    sums_end("d", qd, qd_in, gd)
+    sums_pass("u", qu, qu_in)
     last_gather()
-    sums_send("u", ru, qu, qu_in)
-    sums_pass("u", qu, qu_in)
+    sums_end("u", qu, qu_in, gu)
     lift()
-    sums_end("d", qd, qd_in, gd)
-    sums_end("u", qu, qu_in, gu)
     last_sum()
 
     for copy in sent.values():
@@ -524,7 +569,7 @@
             vmem((ROWS, COLS), F32),
             vmem((4, ROWS, COLS), BF16),
             vmem((4, ROWS, COLS), BF16),
-            vmem((4, HALF, COLS), BF16),
+            vmem((2, ROWS, COLS), BF16),
             vmem((4, 4, 2, 2, HR, FEAT), BF16),
             vmem((4, 4, 2, 2, HR, COLS), BF16),
             vmem((2, NB, HR, FEAT), BF16),

time: 95.4 us -> 87.4 us (0.916)
  Pallas kernels: 91.4 us -> 83.5 us
    pallas_call x1, Pallas kernels: 91.4 us -> 83.5 us  [local(): pl.pallas_call(kernel, name='projections', out_shape=tuple((vmem(s.shape,...]
where the time goes in v3:
time: 87.4 us; the launch traced here: 87.3 us
  Pallas kernels  83.5 us (96%)
  local copies, waits for them, and re-layouts  3.22 us (4%)
    pallas_call x1, Pallas kernels, local(): pl.pallas_call(kernel, name='projections', out_shape=tuple((vmem(s.shape,...  83.5 us
    unnamed x4, local copies, waits for them, and re-layouts  3.22 us

profile of v3, /device:TPU:1, one launch (start us, length us, event | category | flops | bytes accessed | tf_op | source)
XLA Modules:
  0.0 87.3 jit_solution(275915307257098163)
XLA Ops:
  0.6 83.5 %projections.1 = (bf16[768,256]{1,0:T(8,128)(2,1)S(1)}, bf16[768,1024]{1,0:T(8,128)(2,1)S(1)}, bf16[2,64,1024]{2,1,0:T(8,128)(2,1)S(1)}, bf16[2,64,256]{2,1,0:T(8,128)(2,1)S(1)}) custom-call(s32[64]{0:T(128)} %stored.1, s32[6]{0:T(128)} %tenants.1, s32[6]{0:T(128)} %padding.1, bf16[768,1024]{1,0:T(8,128)(2,1)} %tok_in.1, bf16[1024,2048]{1,0:T(8,128)(2,1)} %w_in.1, ...), custom_call_target="tpu_custom_call" | custom-call | tf_op jit(solution)/shard_map/projections/pallas_call | solution.py:557
  84.1 0.7 copy.16
  84.9 0.6 copy.19
  85.5 0.7 copy.18
  86.2 1.1 %copy.17 = bf16[768,1024]{1,0:T(8,128)(2,1)} copy(bf16[768,1024]{1,0:T(8,128)(2,1)S(1)} %get-tuple-element.13) | data formatting | bytes 3145728

commit v4 on v3

--- a/solution.py
+++ b/solution.py
@@ -28,7 +28,7 @@
     ad, au, dh, uh, dx, ux, ints, ints_smem, table,
     low_part, low_recv, low, low_x, back_part, back_recv, back, back_x,
     rd, ru, qd, qu, qd_in, qu_in,
-    send_sem, recv_sem, load_sem, copy_sem,
+    send_sem, recv_sem, load_sem, copy_sem, far_sem,
 ):
     dp, z = lax.axis_index("dp"), lax.axis_index("tensor")
     y, x, c = dp // 8, (dp // 2) % 4, dp % 2
@@ -71,6 +71,12 @@
             arrived.add(key)
             sent[key].wait_recv()
 
+    barrier = pltpu.get_barrier_semaphore()
+    friends = [z_at(1), z_at(-1)] + [p_at(1), p_at(-1), q_at(1), q_at(-1), sibling]
+    friends += [q_cross(1), q_cross(-1)]
+    for friend in friends:
+        pl.semaphore_signal(barrier, inc=1, device_id=friend, device_id_type=MESH)
+
     loads = {}
 
     def load(key, src, dst):
@@ -95,12 +101,6 @@
     for k in (4, 3, 5, 0, 2, 6, 1, 7):
         load(("w", k), w_in.at[:, pl.ds(((z + k) % NZ) * COLS, COLS)], w.at[k])
 
-    barrier = pltpu.get_barrier_semaphore()
-    friends = [z_at(k) for k in range(1, NZ)] + [p_at(1), p_at(-1), q_at(1), q_at(-1), sibling]
-    friends += [q_cross(1), q_cross(-1)]
-    for friend in friends:
-        pl.semaphore_signal(barrier, inc=1, device_id=friend, device_id_type=MESH)
-
     lane = lax.broadcasted_iota(I32, (8, 128), 1)
     tile = jnp.zeros((8, 128), I32)
     for b in range(NB):
@@ -118,6 +118,12 @@
         g[0, rows] = (g[0, rows].astype(F32) * live(b)).astype(BF16)
 
     pl.semaphore_wait(barrier, len(friends))
+
+    def tell(k, step):
+        for way in (step, -step):
+            pl.semaphore_signal(far_sem.at[k], inc=1, device_id=z_at(way), device_id_type=MESH)
+
+    tell(0, 1)
 
     half = [pl.ds(h * PIECE, PIECE) for h in range(PIECES)]
 
@@ -259,6 +265,7 @@
 
     def back_begin():
         pick("u", au, uh, ux)
+        pl.semaphore_wait(far_sem.at[1], 2)
         recv("xg")
         for b in range(NB):
             back_part[rank_rows(0, b)] = mm(uh[0, b], g[0, block(b)], NT).astype(BF16)
@@ -451,6 +458,8 @@
         send("xtok", tok.at[0], tok.at[1], sibling)
 
     def ints_0():
+        pl.semaphore_wait(far_sem.at[0], 2)
+        tell(1, 2)
         recv("f0i")
         send(("i", 1), ints.at[0], ints.at[3], q_at(1))
         send(("i", -1), ints.at[0], ints.at[1], q_at(-1))
@@ -545,6 +554,23 @@
         copy.wait_send()
 
 
+def write(gt, kv, gd, gu, gt_out, kv_out, gd_out, gu_out, sem):
+    copies = []
+
+    def copy(src, dst):
+        copies.append(pltpu.make_async_copy(src, dst, sem.at[len(copies)]))
+        copies[-1].start()
+
+    for k in range(4):
+        rows = pl.ds(k * (ROWS // 4), ROWS // 4)
+        copy(gt.at[rows], gt_out.at[rows])
+    copy(kv, kv_out)
+    copy(gd, gd_out)
+    copy(gu, gu_out)
+    for done in copies:
+        done.wait()
+
+
 def local(tokens, frozen_weight, cotangent, down_maps, up_maps, stored_row, tenants, padding):
     shape = jax.ShapeDtypeStruct
     smem, anywhere = pl.BlockSpec(memory_space=pltpu.SMEM), pl.BlockSpec(memory_space=pl.ANY)
@@ -554,7 +580,7 @@
         shape((ROWS, COLS), BF16), shape((ROWS, FEAT), BF16),
         shape((2, RANK, FEAT), BF16), shape((2, RANK, COLS), BF16),
     )
-    kv, gt, gd, gu = pl.pallas_call(
+    results = pl.pallas_call(
         kernel,
         name="projections",
         out_shape=tuple(vmem(s.shape, s.dtype) for s in shapes),
@@ -597,6 +623,7 @@
             pltpu.SemaphoreType.DMA((N_SEM,)),
             pltpu.SemaphoreType.DMA((16,)),
             pltpu.SemaphoreType.DMA,
+            pltpu.SemaphoreType.REGULAR((2,)),
         ],
         compiler_params=pltpu.CompilerParams(
             collective_id=0, has_side_effects=True, vmem_limit_bytes=60 * 2**20
@@ -605,6 +632,16 @@
         stored_row, tenants, padding, tokens, frozen_weight, cotangent,
         jnp.swapaxes(down_maps, 1, 2), up_maps,
     )
+    kv, gt, gd, gu = results
+    gt, kv, gd, gu = pl.pallas_call(
+        write,
+        name="write",
+        out_shape=(shapes[1], shapes[0], shapes[2], shapes[3]),
+        in_specs=[inside] * 4,
+        out_specs=[anywhere] * 4,
+        scratch_shapes=[pltpu.SemaphoreType.DMA((7,))],
+        compiler_params=pltpu.CompilerParams(vmem_limit_bytes=2 * 2**20),
+    )(gt, kv, gd, gu)
     return kv, gt, jnp.swapaxes(gd, 1, 2), gu
 
 

time: 87.4 us -> 84.9 us (0.971)
  local copies, waits for them, and re-layouts: 3.22 us -> 0 us
    unnamed x4 -> x0, local copies, waits for them, and re-layouts: 3.22 us -> none
    pallas_call x0 -> x1, Pallas kernels: none -> 1.43 us  [local(): pl.pallas_call(write, name='write', out_shape=(shapes[1], shapes[0], shap...]
where the time goes in v4:
time: 84.9 us; the launch traced here: 84.8 us
  Pallas kernels  84.1 us (99%)
    pallas_call x1, Pallas kernels, local(): pl.pallas_call(kernel, name='projections', out_shape=tuple((vmem(s.shape,...  82.7 us

profile of v4, /device:TPU:1, one launch (start us, length us, event | category | flops | bytes accessed | tf_op | source)
XLA Modules:
  0.0 84.8 jit_solution(13518662572301758180)
XLA Ops:
  0.6 82.7 %projections.1 = (bf16[768,256]{1,0:T(8,128)(2,1)S(1)}, bf16[768,1024]{1,0:T(8,128)(2,1)S(1)}, bf16[2,64,1024]{2,1,0:T(8,128)(2,1)S(1)}, bf16[2,64,256]{2,1,0:T(8,128)(2,1)S(1)}) custom-call(s32[64]{0:T(128)} %stored.1, s32[6]{0:T(128)} %tenants.1, s32[6]{0:T(128)} %padding.1, bf16[768,1024]{1,0:T(8,128)(2,1)} %tok_in.1, bf16[1024,2048]{1,0:T(8,128)(2,1)} %w_in.1, ...), custom_call_target="tpu_custom_call" | custom-call | tf_op jit(solution)/shard_map/projections/pallas_call | solution.py:583
  83.3 1.4 %write.1 = (bf16[768,1024]{1,0:T(8,128)(2,1)}, bf16[768,256]{1,0:T(8,128)(2,1)}, bf16[2,64,1024]{2,1,0:T(8,128)(2,1)}, bf16[2,64,256]{2,1,0:T(8,128)(2,1)}) custom-call(bf16[768,1024]{1,0:T(8,128)(2,1)S(1)} %get-tuple-element.12.gt, bf16[768,256]{1,0:T(8,128)(2,1)S(1)} %get-tuple-element.13.kv, bf16[2,64,1024]{2,1,0:T(8,128)(2,1)S(1)} %get-tuple-element.14.gd, ...), custom_call_target="tpu_custom_call" | custom-call | tf_op jit(solution)/shard_map/write/pallas_call | solution.py:636

commit v5 on v4

--- a/solution.py
+++ b/solution.py
@@ -64,7 +64,13 @@
         copy.start()
         sent[key] = copy
 
-    arrived = set()
+    arrived, settled = set(), set()
+
+    def settle(keys):
+        for key in keys:
+            if key not in settled:
+                settled.add(key)
+                sent[key].wait_send()
 
     def recv(key):
         if key not in arrived:
@@ -130,6 +136,9 @@
     def goes_right(h):
         return h < PIECES // 2
 
+    def gathers_right(h):
+        return h < PIECES // 2 - 1
+
     def ag_send(step, h, right):
         src, dst = ((-step) % NZ, (-step - 1) % NZ) if right else (step, step + 1)
         send(("ag", right, step, h), g.at[src, half[h]], g.at[dst, half[h]], z_at(1 if right else -1))
@@ -137,7 +146,7 @@
     def ag_pass(step, h):
         for right in (True, False):
             recv(("ag", right, step, h))
-            if step < 2 or goes_right(h) == right:
+            if step < 2 or gathers_right(h) == right:
                 ag_send(step + 1, h, right)
 
     def partial(k, h):
@@ -405,7 +414,7 @@
     def last_gather():
         wait_w(4)
         for h in range(PIECES):
-            recv(("ag", goes_right(h), 3, h))
+            recv(("ag", gathers_right(h), 3, h))
 
         def body(i, _):
             rows = pl.ds(i * 256, 256)
@@ -509,18 +518,20 @@
     fetch_2("d", ad)
     fetch_4("d", ad)
     rs_pass(1, 3)
+    fill_table()
     sum_gather("back", back_part, back_recv, back, 0.5)
     ag_pass(0, 2)
     ag_pass(0, 0)
     rs_pass(2, 2)
+    first = list(sent)
     fetch_5("d", ad)
     rs_pass(2, 1)
     low_begin()
     down_terms()
     ag_pass(1, 2)
-    fill_table()
     ag_pass(1, 0)
     side()
+    settle(first)
     sum_gather("low", low_part, low_recv, low, 1.0)
     rs_pass(3, 2)
     rs_pass(2, 3)
@@ -534,6 +545,7 @@
     ag_pass(2, 0)
     sums_send("d", rd, qd, qd_in)
     terms_pass("u", ru)
+    lift()
     ag_pass(2, 3)
     ag_pass(2, 2)
     rs_pass(3, 1)
@@ -547,11 +559,9 @@
     sums_pass("u", qu, qu_in)
     last_gather()
     sums_end("u", qu, qu_in, gu)
-    lift()
     last_sum()
 
-    for copy in sent.values():
-        copy.wait_send()
+    settle(list(sent))
 
 
 def write(gt, kv, gd, gu, gt_out, kv_out, gd_out, gu_out, sem):

time: 84.9 us -> 84.1 us (level)
  Pallas kernels: 84.1 us -> 83.2 us
    pallas_call x1, Pallas kernels: 82.7 us -> 81.8 us  [local(): pl.pallas_call(kernel, name='projections', out_shape=tuple((vmem(s.shape,...]
where the time goes in v5:
time: 84.1 us; the launch traced here: 83.9 us
  Pallas kernels  83.2 us (99%)
    pallas_call x1, Pallas kernels, local(): pl.pallas_call(kernel, name='projections', out_shape=tuple((vmem(s.shape,...  81.8 us

profile of v5, /device:TPU:1, one launch (start us, length us, event | category | flops | bytes accessed | tf_op | source)
XLA Modules:
  0.0 83.9 jit_solution(4463859523529771187)
XLA Ops:
  0.6 81.8 %projections.1 = (bf16[768,256]{1,0:T(8,128)(2,1)S(1)}, bf16[768,1024]{1,0:T(8,128)(2,1)S(1)}, bf16[2,64,1024]{2,1,0:T(8,128)(2,1)S(1)}, bf16[2,64,256]{2,1,0:T(8,128)(2,1)S(1)}) custom-call(s32[64]{0:T(128)} %stored.1, s32[6]{0:T(128)} %tenants.1, s32[6]{0:T(128)} %padding.1, bf16[768,1024]{1,0:T(8,128)(2,1)} %tok_in.1, bf16[1024,2048]{1,0:T(8,128)(2,1)} %w_in.1, ...), custom_call_target="tpu_custom_call" | custom-call | tf_op jit(solution)/shard_map/projections/pallas_call | solution.py:593
  82.4 1.4 %write.1 = (bf16[768,1024]{1,0:T(8,128)(2,1)}, bf16[768,256]{1,0:T(8,128)(2,1)}, bf16[2,64,1024]{2,1,0:T(8,128)(2,1)}, bf16[2,64,256]{2,1,0:T(8,128)(2,1)}) custom-call(bf16[768,1024]{1,0:T(8,128)(2,1)S(1)} %get-tuple-element.12.gt, bf16[768,256]{1,0:T(8,128)(2,1)S(1)} %get-tuple-element.13.kv, bf16[2,64,1024]{2,1,0:T(8,128)(2,1)S(1)} %get-tuple-element.14.gd, ...), custom_call_target="tpu_custom_call" | custom-call | tf_op jit(solution)/shard_map/write/pallas_call | solution.py:646
